TPU v7x, 256 devices: a whole 4x4x8 slice. The times are simulated.
256 devices in a mesh: noise: 8 (over z), row: 16 (over y, x), col: 2 (over core).
Axes of the slice: x: 4, y: 4, z: 8, core: 2. Of those that a mesh axis runs over, the one named last changes fastest.
Arguments:
- images: bfloat16 [256, 4, 6144], P('row', None, 'col'), may hold values from -40 to 40
- gain: float32 [6144], P('col'), may hold values from 0.3 to 3.5
- up_weight: bfloat16 [6144, 12288], P('col', 'row'), may hold values from -0.078125 to 0.078125
- down_weight: bfloat16 [12288, 6144], P('row', 'col'), may hold values from -0.0546875 to 0.0546875
- cotangent: bfloat16 [256, 16, 6144], P('row', 'noise', 'col'), may hold values from -6 to 6
- seeds: int32 [16], P('noise'), may hold values from 0 to 999999
- assign: int32 [16, 1], replicated, may hold values from 0 to 3, as said below
Outputs:
- saliency: float32 [256, 4, 6144], P('row', None, 'col')
Inputs may be any that keep to these rules, and one draw needn't show every extreme that they name: `assign`: every one of the 4 images is named by at least one copy.
All inputs are finite; a program needn't handle non-finite values.
Results may differ from a plain program's by a relative error of at most 0.0019.
Values may be sent and summed in bfloat16 or wider, within the bound.
A program may use at most 64 MiB of HBM per device.

v0:
```python
import math

import jax
import jax.numpy as jnp
from jax import lax
from jax.sharding import PartitionSpec as P

D = 6144


noise_scale = 0.6
gelu_coef = 0.044715
root_term = math.sqrt(2.0 / math.pi)


def mix_noise(seed_value, token_index, feature_index, width):
    linear = token_index[:, None] * width + feature_index[None, :]
    mixed = linear * 1664525 + seed_value * 1013904223
    mixed = mixed ^ mixed >> 13
    mixed = mixed * 1274126177
    mixed = mixed ^ mixed >> 16
    return ((mixed & 65535).astype(jnp.float32) - 32767.5) * (1.0 / 18918.0)


def gelu_slope(preact):
    inner = root_term * (preact + gelu_coef * preact * preact * preact)
    tanh_val = jnp.tanh(inner)
    return 0.5 * (1.0 + tanh_val) + 0.5 * preact * (1.0 - tanh_val * tanh_val) * root_term * (
        1.0 + 3.0 * gelu_coef * preact * preact
    )


def body(images, gain, up_weight, down_weight, cotangent, seeds, assign):
    slot_count = seeds.shape[0]
    tok_local = images.shape[0]
    image_count = images.shape[1]
    width_local = images.shape[2]
    col_index = lax.axis_index("col")
    row_index = lax.axis_index("row")
    noise_index = lax.axis_index("noise")
    image_ids = jnp.arange(image_count, dtype=jnp.int32)
    my_images = lax.dynamic_slice_in_dim(assign[:, 0], noise_index * slot_count, slot_count)
    onehot = (my_images[:, None] == image_ids[None, :]).astype(jnp.float32)
    clean_rows = jnp.einsum(
        "si,tid->tsd", onehot.astype(jnp.bfloat16), images, preferred_element_type=jnp.float32
    )
    token_index = row_index * tok_local + jnp.arange(tok_local, dtype=jnp.int32)
    feature_index = col_index * width_local + jnp.arange(width_local, dtype=jnp.int32)
    noise_field = jax.vmap(
        lambda seed_value: mix_noise(seed_value, token_index, feature_index, D), out_axes=1
    )(seeds)
    noisy_rows = clean_rows + noise_scale * noise_field
    feat_mean = lax.psum(jnp.sum(noisy_rows, axis=-1), "col") / D
    centred = noisy_rows - feat_mean[..., None]
    feat_var = lax.psum(jnp.sum(centred * centred, axis=-1), "col") / D
    inv_std = lax.rsqrt(feat_var + 1e-06)[..., None]
    normed = centred * inv_std
    scaled = (normed * gain).astype(jnp.bfloat16)
    gathered = (
        lax.all_gather(scaled, "row", axis=0, tiled=True),
        lax.all_gather(cotangent, "row", axis=0, tiled=True),
    )
    row_count = gathered[0].shape[0] * slot_count
    full_scaled = gathered[0].reshape(row_count, width_local)
    full_cotangent = gathered[1].reshape(row_count, width_local)
    preact_part = jnp.dot(full_scaled, up_weight, preferred_element_type=jnp.float32)
    back_part = jnp.einsum(
        "td,hd->th", full_cotangent, down_weight, preferred_element_type=jnp.float32
    )
    preact, back_grad = lax.psum((preact_part, back_part), "col")
    hidden_grad = (back_grad * gelu_slope(preact)).astype(jnp.bfloat16)
    scaled_grad = lax.psum_scatter(
        jnp.einsum("th,dh->td", hidden_grad, up_weight, preferred_element_type=jnp.float32),
        "row",
        scatter_dimension=0,
        tiled=True,
    )
    scaled_grad = scaled_grad.reshape(tok_local, slot_count, width_local)
    normed_grad = scaled_grad * gain
    grad_sum, grad_dot = lax.psum(
        (jnp.sum(normed_grad, axis=-1), jnp.sum(normed_grad * normed, axis=-1)), "col"
    )
    input_grad = cotangent.astype(jnp.float32) + inv_std * (
        normed_grad - grad_sum[..., None] / D - normed * (grad_dot[..., None] / D)
    )
    partial_totals = jnp.einsum("si,tsd->tid", onehot, input_grad, precision=lax.Precision.HIGHEST)
    onehot_all = (assign[:, 0][:, None] == image_ids[None, :]).astype(jnp.float32)
    counts = jnp.sum(onehot_all, axis=0)
    totals = lax.psum(partial_totals, "noise")
    return totals / counts[None, :, None]


def solution(mesh):
    placed = (
        P("row", None, "col"),
        P("col"),
        P("col", "row"),
        P("row", "col"),
        P("row", "noise", "col"),
        P("noise"),
        P(),
    )
    return jax.shard_map(
        body, mesh=mesh, in_specs=placed, out_specs=P("row", None, "col"), check_vma=False
    )
```

profile of v0, /device:TPU:32, one launch (start us, length us, event | category | flops | bytes accessed | tf_op | source)
XLA Modules:
  0.0 360.7 jit_solution(3402559265118721403)
XLA Ops:
  6.6 0.7 broadcast_multiply_fusion.3
  7.3 0.7 dynamic-slice_bitcast_fusion
  8.1 0.9 fusion.41
  9.0 2.5 psum.49
  11.5 0.4 multiply_reduce_fusion.2
  11.8 2.5 psum.50
  14.3 1.0 multiply_convert_fusion
  15.4 0.7 all-gather.3.cloned.1.call-update
  16.1 54.9 %all-gather.5.cloned.1.call-done = bf16[256,2,3072]{2,1,0:T(2,128)(2,1)} async-done(((bf16[16,2,3072]{2,1,0:T(2,128)(2,1)}), bf16[256,2,3072]{2,1,0:T(2,128)(2,1)}) %all-gather.5.cloned.1.call-update) | async-done | bytes 3145744 | tf_op jit(solution)/shard_map/all_gather | solution.py:60
  71.0 7.5 %reshape.60 = bf16[512,3072]{1,0:T(8,128)(2,1)} reshape(bf16[256,2,3072]{2,1,0:T(2,128)(2,1)} %all-gather.5.cloned.1.call-done) | data formatting | bytes 6291456 | tf_op jit(solution)/shard_map/reshape | solution.py:64
  78.6 7.1 %fusion.43 = f32[512,768]{1,0:T(8,128)} fusion(bf16[512,3072]{1,0:T(8,128)(2,1)} %reshape.60, bf16[3072,768]{1,0:T(8,128)(2,1)} %param.9), kind=kOutput, calls=%fused_computation.66 | convolution fusion | flops 2415919104 | bytes 9437184 | tf_op jit(solution)/shard_map/dot_general | solution.py:66
  85.6 39.8 %all-gather.3.cloned.1.call-done = bf16[256,2,3072]{2,1,0:T(2,128)(2,1)} async-done(((bf16[16,2,3072]{2,1,0:T(2,128)(2,1)}), bf16[256,2,3072]{2,1,0:T(2,128)(2,1)}) %all-gather.3.cloned.1.call-update) | async-done | bytes 3145744 | tf_op jit(solution)/shard_map/all_gather | solution.py:61
  125.4 7.5 %reshape.59 = bf16[512,3072]{1,0:T(8,128)(2,1)} reshape(bf16[256,2,3072]{2,1,0:T(2,128)(2,1)} %all-gather.3.cloned.1.call-done) | data formatting | bytes 6291456 | tf_op jit(solution)/shard_map/reshape | solution.py:65
  133.0 7.1 %fusion.42 = f32[512,768]{1,0:T(8,128)} fusion(bf16[512,3072]{1,0:T(8,128)(2,1)} %reshape.59, bf16[768,3072]{1,0:T(8,128)(2,1)} %param.10), kind=kOutput, calls=%fused_computation.65 | convolution fusion | flops 2415919104 | bytes 9437184 | tf_op jit(solution)/shard_map/td,hd->th/dot_general | solution.py:67
  140.1 33.1 %all-reduce.7.cloned.1.call-done = (f32[512,768]{1,0:T(8,128)}, f32[512,768]{1,0:T(8,128)}) async-done(((f32[512,768]{1,0:T(8,128)}, f32[512,768]{1,0:T(8,128)}), (f32[512,768]{1,0:T(8,128)}, f32[512,768]{1,0:T(8,128)})) %all-reduce.7.cloned.1.call-update) | async-done | bytes 3145744 | tf_op jit(solution)/shard_map/psum | solution.py:70
  173.3 9.2 %fusion.8 = f32[512,3072]{1,0:T(8,128)} fusion(bf16[3072,768]{1,0:T(8,128)(2,1)} %param.9, f32[512,768]{1,0:T(8,128)} %get-tuple-element.7, f32[512,768]{1,0:T(8,128)} %get-tuple-element.8), kind=kOutput, calls=%fused_computation.12 | convolution fusion | flops 2423390208 | bytes 14155776 | tf_op jit(solution)/shard_map/th,dh->td/dot_general | solution.py:73
  182.5 0.2 all-reduce.5.cloned.1.call-start
  182.7 87.6 %reduce-scatter.2.cloned.1.call-done = f32[32,3072]{1,0:T(8,128)} async-done(((f32[512,3072]{1,0:T(8,128)}), f32[32,3072]{1,0:T(8,128)}) %reduce-scatter.2.cloned.1.call-update) | async-done | bytes 393232 | tf_op jit(solution)/shard_map/reduce_scatter | solution.py:72
  270.3 1.3 reshape.61
  271.6 0.5 multiply_reduce_fusion
  272.3 3.3 all-reduce
  275.6 2.3 convolution_bitcast_fusion
  278.1 73.9 %all-reduce.5.cloned.1.call-done = f32[16,4,3072]{2,1,0:T(4,128)} async-done(((f32[16,4,3072]{2,1,0:T(4,128)}), f32[16,4,3072]{2,1,0:T(4,128)}) %all-reduce.5.cloned.1.call-update) | async-done | bytes 786448 | tf_op jit(solution)/shard_map/psum | solution.py:89
  351.9 2.3 broadcast_divide_fusion
  (27 shorter events, 0.7 us)
Async XLA Ops:
  6.5 1.5 copy-start
  6.5 64.5 %all-gather.5.cloned.1.call-start = ((), (), s32[]{:S(2)}) async-start(), calls=%async_computation.2 | async-start | bytes 3342336 | tf_op jit(solution)/shard_map/all_gather | solution.py:60
  8.1 6.2 %copy-start.3 = (f32[3072]{0:T(1024)S(1)}, f32[3072]{0:T(1024)}, u32[]{:S(2)}) copy-start(f32[3072]{0:T(1024)} %param.8) | copy-start | bytes 36868
  15.3 110.1 %all-gather.3.cloned.1.call-start = ((), (), s32[]{:S(2)}) async-start(), calls=%async_computation.1 | async-start | bytes 3342336 | tf_op jit(solution)/shard_map/all_gather | solution.py:61
  16.1 157.2 %all-reduce.7.cloned.1.call-start = ((), (), s32[]{:S(2)}) async-start(), calls=%async_computation.5 | async-start | bytes 6291456 | tf_op jit(solution)/shard_map/psum | solution.py:70
  140.1 130.2 %reduce-scatter.2.cloned.1.call-start = ((), (), s32[]{:S(2)}) async-start(), calls=%async_computation.3 | async-start | bytes 6684672 | tf_op jit(solution)/shard_map/reduce_scatter | solution.py:72
  182.5 93.1 %copy-start.2 = (bf16[16,2,3072]{2,1,0:T(2,128)(2,1)S(1)}, bf16[16,2,3072]{2,1,0:T(2,128)(2,1)}, u32[]{:S(2)}) copy-start(bf16[16,2,3072]{2,1,0:T(2,128)(2,1)} %param.11) | copy-start | bytes 589828
  182.5 169.5 %all-reduce.5.cloned.1.call-start = ((), (), s32[]{:S(2)}) async-start(), calls=%async_computation.4 | async-start | bytes 1572864 | tf_op jit(solution)/shard_map/psum | solution.py:89
  270.3 1.8 copy-start.1
  275.6 2.4 copy-start.4
Sparse Core Ops, SparseCore 0:
  15.4 55.5 all-gather.4
  73.5 51.9 all-gather.2
  140.2 33.0 all-reduce.6
  182.6 87.6 reduce-scatter.1
  278.1 73.8 all-reduce.4
where the time goes:
time: 362 us; the launch traced here: 361 us
  waiting for transfers between devices  290 us (80%)
  matrix products  26.6 us (7%)
  local copies, waits for them, and re-layouts  17.2 us (5%)
  between operations  13.2 us (4%)
  blocking collectives  8.21 us (2%)
  other arithmetic  5.16 us (1%)
    reduce_scatter x1, waiting for transfers between devices, body(): lax.psum_scatter(jnp.einsum('th,dh->td', hidden_grad, up_weight, preferre...  87.6 us
    psum x1, waiting for transfers between devices, body(): totals = lax.psum(partial_totals, 'noise')  73.9 us
    all_gather x1, waiting for transfers between devices, body(): lax.all_gather(scaled, 'row', axis=0, tiled=True)  54.9 us
    all_gather x1, waiting for transfers between devices, body(): lax.all_gather(cotangent, 'row', axis=0, tiled=True)  39.8 us
    psum x1, waiting for transfers between devices, body(): preact, back_grad = lax.psum((preact_part, back_part), 'col')  33.1 us
    dot_general x1, matrix products, body(): jnp.einsum('th,dh->td', hidden_grad, up_weight, preferred_element_type=jn...  9.19 us
    reshape x1, local copies, waits for them, and re-layouts, body(): full_scaled = gathered[0].reshape(row_count, width_local)  7.54 us
    reshape x1, local copies, waits for them, and re-layouts, body(): full_cotangent = gathered[1].reshape(row_count, width_local)  7.51 us
  transfers between devices with their start and end apart: 5, of which 5 were waited for; matrix products, arithmetic and copies ran while one was open for 4% of the time, Pallas kernels for 0%

commit v1 on v0

v1 whole, which is shorter than its diff:
```python
import math

import jax
import jax.numpy as jnp
from jax import lax
from jax.sharding import PartitionSpec as P

D = 6144

noise_scale = 0.6
gelu_coef = 0.044715
root_term = math.sqrt(2.0 / math.pi)


def mix_noise(seed_value, token_index, feature_index, width):
    linear = token_index[:, None] * width + feature_index[None, :]
    mixed = linear * 1664525 + seed_value * 1013904223
    mixed = mixed ^ mixed >> 13
    mixed = mixed * 1274126177
    mixed = mixed ^ mixed >> 16
    return ((mixed & 65535).astype(jnp.float32) - 32767.5) * (1.0 / 18918.0)


def gelu_slope(preact):
    inner = root_term * (preact + gelu_coef * preact * preact * preact)
    tanh_val = jnp.tanh(inner)
    return 0.5 * (1.0 + tanh_val) + 0.5 * preact * (1.0 - tanh_val * tanh_val) * root_term * (
        1.0 + 3.0 * gelu_coef * preact * preact
    )


def body(images, gain, up_weight, down_weight, cotangent, seeds, assign):
    tok_local = images.shape[0]
    image_count = images.shape[1]
    width_local = images.shape[2]
    planes = lax.axis_size("noise")
    rows = lax.axis_size("row")
    part = tok_local // planes
    col_index = lax.axis_index("col")
    row_index = lax.axis_index("row")
    noise_index = lax.axis_index("noise")
    all_seeds = lax.all_gather(seeds, "noise", tiled=True)
    slots = all_seeds.shape[0]
    own_cot = lax.all_to_all(cotangent, "noise", split_axis=0, concat_axis=1, tiled=True)
    own_images = lax.dynamic_slice_in_dim(images, noise_index * part, part)
    plane_images = lax.all_gather(own_images, "row", axis=0, tiled=True)
    plane_cot = lax.all_gather(own_cot, "row", axis=0, tiled=True)

    image_ids = jnp.arange(image_count, dtype=jnp.int32)
    onehot = (assign[:, 0][:, None] == image_ids[None, :]).astype(jnp.float32)
    counts = jnp.sum(onehot, axis=0)
    clean = jnp.einsum(
        "si,tid->tsd", onehot.astype(jnp.bfloat16), plane_images, preferred_element_type=jnp.float32
    )
    tokens = (
        jnp.arange(rows, dtype=jnp.int32)[:, None] * tok_local
        + noise_index * part
        + jnp.arange(part, dtype=jnp.int32)[None, :]
    ).reshape(-1)
    feature_index = col_index * width_local + jnp.arange(width_local, dtype=jnp.int32)
    noise_field = jax.vmap(
        lambda seed_value: mix_noise(seed_value, tokens, feature_index, D), out_axes=1
    )(all_seeds)
    noisy = clean + noise_scale * noise_field
    feat_mean = lax.psum(jnp.sum(noisy, axis=-1), "col") / D
    centred = noisy - feat_mean[..., None]
    feat_var = lax.psum(jnp.sum(centred * centred, axis=-1), "col") / D
    inv_std = lax.rsqrt(feat_var + 1e-06)
    normed = centred * inv_std[..., None]
    scaled = (normed * gain).astype(jnp.bfloat16)
    n = tokens.shape[0] * slots
    preact_part = jnp.dot(scaled.reshape(n, width_local), up_weight, preferred_element_type=jnp.float32)
    back_part = jnp.einsum(
        "td,hd->th", plane_cot.reshape(n, width_local), down_weight, preferred_element_type=jnp.float32
    )
    ug_part = jnp.sum(gain[:, None] * up_weight.astype(jnp.float32), axis=0)
    preact, back_grad, ug = lax.psum((preact_part, back_part, ug_part), "col")
    hidden_grad = (back_grad * gelu_slope(preact)).astype(jnp.bfloat16)
    hg = hidden_grad.astype(jnp.float32)
    sums = jnp.stack([jnp.sum(hg * ug, axis=-1), jnp.sum(hg * preact, axis=-1)], axis=-1) / D
    sums = lax.psum_scatter(sums.reshape(-1, slots, 2), "row", scatter_dimension=0, tiled=True)
    weighted = jnp.einsum(
        "ts,si,tsh->tih", inv_std, onehot, hg.reshape(-1, slots, hg.shape[-1]),
        precision=lax.Precision.HIGHEST,
    ).astype(jnp.bfloat16)
    grad = jnp.einsum(
        "th,dh->td", weighted.reshape(-1, hg.shape[-1]), up_weight, preferred_element_type=jnp.float32
    )
    grad = lax.psum_scatter(
        grad.reshape(-1, image_count, width_local), "row", scatter_dimension=0, tiled=True
    )
    own_normed = lax.dynamic_slice_in_dim(normed, row_index * part, part)
    own_inv = lax.dynamic_slice_in_dim(inv_std, row_index * part, part)
    rest = own_cot.astype(jnp.float32) - own_inv[..., None] * (
        sums[..., 0][..., None] + own_normed * sums[..., 1][..., None]
    )
    total = grad * gain + jnp.einsum("si,tsd->tid", onehot, rest, precision=lax.Precision.HIGHEST)
    total = total / counts[None, :, None]
    return lax.all_gather(total, "noise", axis=0, tiled=True)


def solution(mesh):
    placed = (
        P("row", None, "col"),
        P("col"),
        P("col", "row"),
        P("row", "col"),
        P("row", "noise", "col"),
        P("noise"),
        P(),
    )
    return jax.shard_map(
        body, mesh=mesh, in_specs=placed, out_specs=P("row", None, "col"), check_vma=False
    )
```

time: 362 us -> 282 us (0.78)
  waiting for transfers between devices: 290 us -> 57 us
  blocking collectives: 8.21 us -> 161 us
  other arithmetic: 5.16 us -> 17.8 us
  local copies, waits for them, and re-layouts: 17.2 us -> 7.18 us
  matrix products: 26.6 us -> 22.1 us
    all_gather x2 -> x1, waiting for transfers between devices: 94.7 us -> 0.01 us  [body(): plane_cot = lax.all_gather(own_cot, 'row', axis=0, tiled=True)]
    reduce_scatter x1 -> x0, waiting for transfers between devices: 87.6 us -> none  [body(): lax.psum_scatter(jnp.einsum('th,dh->td', hidden_grad, up_weight, preferre...]
    unnamed x0 -> x2, blocking collectives: none -> 84.3 us
    psum x2 -> x1, waiting for transfers between devices: 107 us -> 32.9 us  [body(): preact, back_grad, ug = lax.psum((preact_part, back_part, ug_part), 'col')]
    all_gather x0 -> x2, blocking collectives: none -> 52.1 us  [the longest x1 26.6 us: body(): return lax.all_gather(total, 'noise', axis=0, tiled=True)]
    unnamed x5 -> x4, waiting for transfers between devices: 0.76 us -> 24.1 us
    all_to_all x0 -> x1, blocking collectives: none -> 17.7 us  [body(): lax.all_to_all(cotangent, 'noise', split_axis=0, concat_axis=1, tiled=True)]
    reshape x3 -> x0, local copies, waits for them, and re-layouts: 16.3 us -> none  [the longest x1 7.54 us: body(): full_scaled = gathered[0].reshape(row_count, width_local)]
  transfers between devices with their start and end apart: 5 -> 3, of which waited for: 5 -> 2; matrix products, arithmetic and copies ran while one was open for 4% -> 10% of each run, Pallas kernels for 0% -> 0%
where the time goes in v1:
time: 282 us; the launch traced here: 280 us
  blocking collectives  161 us (57%)
  waiting for transfers between devices  57 us (20%)
  matrix products  22.1 us (8%)
  other arithmetic  17.8 us (6%)
  between operations  14.6 us (5%)
  local copies, waits for them, and re-layouts  7.18 us (3%)
    unnamed x2, blocking collectives  84.3 us
    psum x1, waiting for transfers between devices, body(): preact, back_grad, ug = lax.psum((preact_part, back_part, ug_part), 'col')  32.9 us
    all_gather x1, blocking collectives, body(): return lax.all_gather(total, 'noise', axis=0, tiled=True)  26.6 us
    all_gather x1, blocking collectives, body(): plane_images = lax.all_gather(own_images, 'row', axis=0, tiled=True)  25.5 us
    unnamed x4, waiting for transfers between devices  24.1 us
    all_to_all x1, blocking collectives, body(): lax.all_to_all(cotangent, 'noise', split_axis=0, concat_axis=1, tiled=True)  17.7 us
    convert_element_type x1, other arithmetic, body(): scaled = (normed * gain).astype(jnp.bfloat16)  7.28 us
    dot_general x1, matrix products, body(): jnp.einsum('td,hd->th', plane_cot.reshape(n, width_local), down_weight, p...  7.09 us
  transfers between devices with their start and end apart: 3, of which 2 were waited for; matrix products, arithmetic and copies ran while one was open for 10% of the time, Pallas kernels for 0%

profile of v1, /device:TPU:32, one launch (start us, length us, event | category | flops | bytes accessed | tf_op | source)
XLA Modules:
  0.0 280.1 jit_solution(14509511110187522334)
XLA Ops:
  6.5 17.7 %all_to_all.18 = bf16[16,2,3072]{2,1,0:T(2,128)(2,1)S(1)} all-to-all(bf16[16,2,3072]{2,1,0:T(2,128)(2,1)} %param.11), channel_id=1, replica_groups=mesh['noise'=8,'row'=16,'col'=2] {'noise'}, dimensions={0} | all-to-all | bytes 393216 | tf_op jit(solution)/shard_map/all_to_all | solution.py:44
  24.4 0.8 all_to_all.16
  25.4 1.3 dynamic-slice
  27.5 0.9 dynamic-update-slice
  28.3 9.7 %all-reduce = s32[16]{0:T(128)S(1)} all-reduce(s32[16]{0:T(128)S(1)} %dynamic-update-slice), channel_id=1, replica_groups=mesh['noise'=8,'row'=16,'col'=2] {'noise'}, use_global_device_ids=true, to_apply=%add | all-reduce | flops 16 | bytes 128
  38.1 25.5 %all_gather.12 = bf16[32,4,3072]{2,1,0:T(4,128)(2,1)S(1)} all-gather(bf16[2,4,3072]{2,1,0:T(4,128)(2,1)S(1)} %constant_dynamic-slice_fusion.1), channel_id=1, replica_groups=mesh['noise'=8,'row'=16,'col'=2] {'row'}, dimensions={0}, use_global_device_ids=true | all-gather | bytes 835584 | tf_op jit(solution)/shard_map/all_gather | solution.py:46
  63.6 5.3 %fusion.44 = (f32[32,16]{1,0:T(8,128)S(1)}, f32[32,16,3072]{2,1,0:T(8,128)}) fusion(s32[16]{0:T(128)S(1)} %broadcast_multiply_fusion.1, s32[32,3072]{1,0:T(8,128)S(1)} %add_multiply_fusion, bf16[32,4,3072]{2,1,0:T(4,128)(2,1)S(1)} %all_gather.12, s32[16]{0:T(128)} %bitcast.49), kind=kOutput, calls=%fused_computation.68 | convolution fusion | flops 31456960 | bytes 7473280 | tf_op jit(solution)/shard_map/si,tid->tsd/dot_general | solution.py:52
  68.9 3.5 %psum.35 = f32[32,16]{1,0:T(8,128)S(1)} all-reduce(f32[32,16]{1,0:T(8,128)S(1)} %get-tuple-element.18), channel_id=1, replica_groups=mesh['noise'=8,'row'=16,'col'=2] {'col'}, use_global_device_ids=true, to_apply=%region_1.0 | all-reduce | flops 512 | bytes 4096 | tf_op jit(solution)/shard_map/psum | solution.py:65
  72.4 3.6 %multiply_reduce_fusion.1 = f32[32,16]{1,0:T(8,128)S(1)} fusion(f32[32,16,3072]{2,1,0:T(8,128)} %get-tuple-element.19, f32[32,16]{1,0:T(8,128)S(1)} %broadcast_multiply_fusion), kind=kLoop, calls=%fused_computation.10 | loop fusion | flops 4718080 | bytes 6295552 | tf_op jit(solution)/shard_map/reduce_sum | solution.py:67
  76.0 3.4 %multiply_reduce_fusion = f32[768]{0:T(1024)S(1)} fusion(bf16[3072,768]{1,0:T(8,128)(2,1)} %param.9, f32[3072]{0:T(1024)S(1)} %copy-done.2), kind=kLoop, calls=%fused_computation.2 | loop fusion | flops 7077120 | bytes 4733952 | tf_op jit(solution)/shard_map/reduce_sum | solution.py:76
  79.4 3.5 %all-reduce.3 = (f32[32,16]{1,0:T(8,128)S(1)}, f32[768]{0:T(1024)S(1)}) all-reduce(f32[32,16]{1,0:T(8,128)S(1)} %multiply_reduce_fusion.1, f32[768]{0:T(1024)S(1)} %multiply_reduce_fusion), channel_id=1, replica_groups=mesh['noise'=8,'row'=16,'col'=2] {'col'}, use_global_device_ids=true, to_apply=%region_3.0 | all-reduce | flops 1280 | bytes 10240 | tf_op jit(solution)/shard_map/psum | solution.py:67
  83.0 7.3 %multiply_convert_fusion = (bf16[32,16,3072]{2,1,0:T(8,128)(2,1)S(1)}, f32[32,16,3072]{2,1,0:T(8,128)}) fusion(f32[3072]{0:T(1024)S(1)} %copy-done.2, f32[32,16]{1,0:T(8,128)S(1)} %get-tuple-element.17, f32[32,16,3072]{2,1,0:T(8,128)} %get-tuple-element.19, f32[32,16]{1,0:T(8,128)S(1)} %broadcast_multiply_fusion), kind=kLoop, calls=%fused_computation.9 | loop fusion | flops 6291456 | bytes 15745024 | tf_op jit(solution)/shard_map/convert_element_type | solution.py:70
  90.3 3.8 %fusion.46 = f32[512,768]{1,0:T(8,128)} fusion(bf16[512,3072]{1,0:T(8,128)(2,1)S(1)} %bitcast.46, bf16[3072,768]{1,0:T(8,128)(2,1)S(1)} %bitcast.44), kind=kOutput, calls=%fused_computation.70 | convolution fusion | flops 2415919104 | bytes 9437184 | tf_op jit(solution)/shard_map/dot_general | solution.py:72
  94.1 7.1 %fusion.45 = f32[512,768]{1,0:T(8,128)} fusion(bf16[512,3072]{1,0:T(8,128)(2,1)} %bitcast.53, bf16[768,3072]{1,0:T(8,128)(2,1)} %param.10), kind=kOutput, calls=%fused_computation.69 | convolution fusion | flops 2415919104 | bytes 9437184 | tf_op jit(solution)/shard_map/td,hd->th/dot_general | solution.py:73
  101.5 32.9 %all-reduce.10.cloned.1.call-done = (f32[512,768]{1,0:T(8,128)}, f32[512,768]{1,0:T(8,128)}) async-done(((f32[512,768]{1,0:T(8,128)}, f32[512,768]{1,0:T(8,128)}), (f32[512,768]{1,0:T(8,128)}, f32[512,768]{1,0:T(8,128)})) %all-reduce.10.cloned.1.call-update) | async-done | bytes 3145744 | tf_op jit(solution)/shard_map/psum | solution.py:77
  134.4 3.2 %fusion.10 = (f32[512]{0:T(512)S(1)}, f32[512]{0:T(512)S(1)}, bf16[512,768]{1,0:T(8,128)(2,1)S(1)}) fusion(f32[768]{0:T(1024)S(1)} %get-tuple-element.8, f32[512,768]{1,0:T(8,128)} %get-tuple-element.10, f32[512,768]{1,0:T(8,128)} %get-tuple-element.9), kind=kLoop, calls=%fused_computation.21 | loop fusion | flops 9436160 | bytes 3939328 | tf_op jit(solution)/shard_map/reduce_sum | solution.py:80
  138.0 4.0 %fusion.6 = f32[32,4,3072]{2,0,1:T(8,128)S(1)} fusion(bf16[3072,768]{1,0:T(8,128)(2,1)} %param.9, bf16[32,4,768]{2,1,0:T(4,128)(2,1)S(1)} %convolution_convert_fusion), kind=kOutput, calls=%fused_computation.12 | convolution fusion | flops 603979776 | bytes 6488064 | tf_op jit(solution)/shard_map/th,dh->td/dot_general | solution.py:86
  142.0 2.2 copy.20
  144.3 0.6 dynamic-slice.1
  145.9 74.6 %all-reduce.2 = f32[32,16,2]{1,0,2:T(8,128)S(1)} all-reduce(f32[32,16,2]{1,0,2:T(8,128)S(1)} %maximum_multiply_fusion), channel_id=3, replica_groups=mesh['noise'=8,'row'=16,'col'=2] {'row'}, use_global_device_ids=true, to_apply=%region_11.0.clone | all-reduce | flops 1024 | bytes 8192
  220.5 24.1 %all-reduce.8.cloned.1.call-done = f32[32,4,3072]{2,1,0:T(4,128)} async-done(((f32[32,4,3072]{2,1,0:T(4,128)}), f32[32,4,3072]{2,1,0:T(4,128)}) %all-reduce.8.cloned.1.call-update) | async-done | bytes 1572880
  244.6 1.4 fusion.9
  246.0 26.6 %all_gather.15 = f32[16,4,3072]{2,1,0:T(4,128)S(1)} all-gather(f32[2,4,3072]{2,1,0:T(4,128)S(1)} %fusion.9), channel_id=1, replica_groups=mesh['noise'=8,'row'=16,'col'=2] {'noise'}, dimensions={0}, use_global_device_ids=true | all-gather | bytes 884736 | tf_op jit(solution)/shard_map/all_gather | solution.py:99
  272.6 0.9 copy.32
  (41 shorter events, 1.6 us)
Async XLA Ops:
  6.5 31.5 %copy-start = (bf16[16,4,3072]{2,1,0:T(4,128)(2,1)S(1)}, bf16[16,4,3072]{2,1,0:T(4,128)(2,1)}, u32[]{:S(2)}) copy-start(bf16[16,4,3072]{2,1,0:T(4,128)(2,1)} %param.7) | copy-start | bytes 1179652
  6.5 87.6 %all-gather.2.cloned.1.call-start = ((), (), s32[]{:S(2)}) async-start(), calls=%async_computation.1 | async-start | bytes 3342336 | tf_op jit(solution)/shard_map/all_gather | solution.py:47
  25.2 109.2 %all-reduce.10.cloned.1.call-start = ((), (), s32[]{:S(2)}) async-start(), calls=%async_computation.3 | async-start | bytes 6291456 | tf_op jit(solution)/shard_map/psum | solution.py:77
  68.9 7.1 %copy-start.2 = (f32[3072]{0:T(1024)S(1)}, f32[3072]{0:T(1024)}, u32[]{:S(2)}) copy-start(f32[3072]{0:T(1024)} %param.8) | copy-start | bytes 36868
  76.0 14.2 %slice-start = ((s8[4718592]{0:T(1024)(128)(4,1)}), s8[524288]{0:T(1024)(128)(4,1)S(1)}, s32[]{:S(2)}) async-start(s8[4718592]{0:T(1024)(128)(4,1)} %bitcast.43), calls=%async_computation.4 | async-start | bytes 1048576
  83.0 7.3 %slice-start.1 = ((s8[4718592]{0:T(1024)(128)(4,1)}), s8[4194304]{0:T(1024)(128)(4,1)S(1)}, s32[]{:S(2)}) async-start(s8[4718592]{0:T(1024)(128)(4,1)} %bitcast.43), calls=%async_computation.5 | async-start | bytes 8388608
  94.1 7.3 %copy-start.3 = (s32[16,1]{0,1:T(1,128)S(1)}, s32[16,1]{0,1:T(1,128)}, u32[]{:S(2)}) copy-start(s32[16,1]{0,1:T(1,128)} %param.13) | copy-start | bytes 196
  101.2 143.4 %all-reduce.8.cloned.1.call-start = ((), (), s32[]{:S(2)}) async-start(), calls=%async_computation.2 | async-start | bytes 3145728
  138.0 6.3 %copy-start.4 = (u32[256]{0:T(256)S(1)}, u32[256]{0:T(256)}, u32[]{:S(2)}) copy-start(u32[256]{0:T(256)} %constant.75) | copy-start | bytes 3076
  138.0 106.6 %copy-start.1 = (bf16[2,16,3072]{2,1,0:T(8,128)(2,1)S(1)}, bf16[2,16,3072]{2,1,0:T(8,128)(2,1)}, u32[]{:S(2)}) copy-start(bf16[2,16,3072]{2,1,0:T(8,128)(2,1)} %all_to_all.16) | copy-start | bytes 589828
Sparse Core Ops, SparseCore 0:
  25.3 51.0 all-gather.1
  101.3 32.9 all-reduce.9
  144.4 100.1 all-reduce.7

commit v2 on v0

v2 whole, which is shorter than its diff:
```python
import math

import jax
import jax.numpy as jnp
from jax import lax
from jax.experimental import pallas as pl
from jax.experimental.pallas import tpu as pltpu
from jax.sharding import PartitionSpec as P

D = 6144
NCH = 6
noise_scale = 0.6
gelu_coef = 0.044715
root_term = math.sqrt(2.0 / math.pi)
MESH = pl.DeviceIdType.MESH
F32 = jnp.float32
BF16 = jnp.bfloat16
I32 = jnp.int32


def gelu_slope(preact):
    inner = root_term * (preact + gelu_coef * preact * preact * preact)
    tanh_val = jnp.tanh(inner)
    return 0.5 * (1.0 + tanh_val) + 0.5 * preact * (1.0 - tanh_val * tanh_val) * root_term * (
        1.0 + 3.0 * gelu_coef * preact * preact
    )


def dot_nt(a, b):
    return lax.dot_general(a, b, (((1,), (1,)), ((), ())), preferred_element_type=F32)


def dot_nn(a, b):
    return lax.dot_general(a, b, (((1,), (0,)), ((), ())), preferred_element_type=F32)


def wrap(i, n):
    return lax.rem(i + n, n)


def kernel(
    img_hbm, gain_ref, up_hbm, dn_hbm, cot_hbm, seeds_ref, assign_ref, out_hbm,
    up_v, dn_v, img_own, pk16, imgg, rc, seedg, pk32, cg, onehot, base, noisy, scl,
    pre, pre_in, ugp, ug_in, slope, bk, bk_in, stat, stat_in, mi, gst, gst_in, wt, wm, wx, wx_in, wall,
    o_s, rs, rr1, ss, rr2, gx, gx_in, gy, gy_in, oh8, out_v,
    load_sem, z_send, z_recv, s_send, s_recv, i_send, i_recv, c_send, c_recv, k_send, k_recv,
    r_send, r_recv, g_send, g_recv, o_send, o_recv,
):
    W = 3072 // NCH
    z = lax.axis_index("noise")
    r = lax.axis_index("row")
    c = lax.axis_index("col")
    y, x = r // 4, lax.rem(r, 4)
    p1 = (x, y)
    p2 = (y, x)

    def row_peer(ab, phase, step):
        along_x = (ab == 0) == (phase == 1)
        if along_x:
            return {"row": y * 4 + wrap(x + step, 4)}
        return {"row": wrap(y + step, 4) * 4 + x}

    def z_peer(step):
        return {"noise": wrap(z + step, 8)}

    other = {"col": 1 - c}

    def rcopy(src, dst, ssem, rsem, dev):
        return pltpu.make_async_remote_copy(
            src_ref=src, dst_ref=dst, send_sem=ssem, recv_sem=rsem, device_id=dev, device_id_type=MESH
        )

    ld_img = pltpu.make_async_copy(img_hbm.at[pl.ds(2 * z, 2)], img_own, load_sem.at[0])
    ld_img.start()
    ld_cot = pltpu.make_async_copy(cot_hbm.at[pl.ds(2 * z, 2)], rc.at[z], load_sem.at[1])
    ld_cot.start()
    ld_up = pltpu.make_async_copy(up_hbm, up_v, load_sem.at[2])
    ld_up.start()
    ld_dn = pltpu.make_async_copy(dn_hbm, dn_v, load_sem.at[3])
    ld_dn.start()

    barrier = pltpu.get_barrier_semaphore()
    for dev in (
        [z_peer(s) for s in range(1, 8)]
        + [row_peer(0, 1, s) for s in (1, 2, 3)]
        + [row_peer(0, 2, s) for s in (1, 2, 3)]
        + [other]
    ):
        pl.semaphore_signal(barrier, inc=1, device_id=dev, device_id_type=MESH)

    seedg[z] = jnp.where(
        lax.broadcasted_iota(I32, (8, 128), 0) == 0, seeds_ref[0], seeds_ref[1]
    )
    ld_img.wait()
    for tok in range(2):
        v = img_own[tok].astype(F32)
        for q in range(4):
            ab, half = q // 2, q % 2
            pk16[half * 8 + tok * 4 : half * 8 + tok * 4 + 4, ab * 768 : (ab + 1) * 768] = v[
                :, q * 768 : (q + 1) * 768
            ]
    for ch in range(2):
        for ab in range(2):
            lo = ab * 768 + ch * 384
            imgg[ch, ab, p2[ab], p1[ab]] = pk16[:, lo : lo + 384].astype(BF16)
    pl.semaphore_wait(barrier, 14)

    sends = []
    z_order = (1, 7, 2, 6, 3, 5, 4)
    for s in z_order:
        peer = wrap(z + s, 8)
        cp = rcopy(cot_hbm.at[pl.ds(2 * peer, 2)], rc.at[z], z_send.at[s], z_recv.at[s], z_peer(s))
        cp.start()
        sends.append(cp)
        cp = rcopy(seedg.at[z], seedg.at[z], s_send.at[s], s_recv.at[s], z_peer(s))
        cp.start()
        sends.append(cp)

    class Gather:
        def __init__(self, buf, ssem, rsem, parity):
            self.buf, self.ssem, self.rsem, self.parity = buf, ssem, rsem, parity

        def blk(self, ab, a, b):
            return self.buf.at[ab, a, b]

        def ring(self, ab, phase):
            me = (p1 if phase == 1 else p2)[ab]

            def at(i):
                i = wrap(me + i, 4)
                return self.buf.at[ab, p2[ab], i] if phase == 1 else self.buf.at[ab, i]

            def mk(i, n, step):
                k = (ab * 2 + phase - 1) * 3 + n
                return rcopy(at(i), at(i), self.ssem.at[k], self.rsem.at[k], row_peer(ab, phase, step))

            right, left = mk(0, 0, 1), mk(0, 1, -1)
            fwd = mk(-1, 2, 1) if self.parity == 0 else mk(1, 2, -1)
            return right, left, fwd

        def first(self, phase):
            for ab in range(2):
                right, left, _ = self.ring(ab, phase)
                right.start()
                left.start()

        def second(self, phase):
            for ab in range(2):
                right, left, fwd = self.ring(ab, phase)
                right.wait_recv()
                left.wait_recv()
                fwd.start()

        def end(self, phase):
            for ab in range(2):
                self.ring(ab, phase)[2].wait_recv()

        def drain(self):
            for ab in range(2):
                for phase in (1, 2):
                    for cp in self.ring(ab, phase):
                        cp.wait_send()

    img_g = [Gather(imgg.at[ch], i_send.at[ch], i_recv.at[ch], ch) for ch in range(2)]
    cot_g = [Gather(cg.at[j], c_send.at[j], c_recv.at[j], j % 2) for j in range(NCH)]

    for g in img_g:
        g.first(1)

    sub16 = lax.broadcasted_iota(I32, (16, 128), 0)
    lane = lax.broadcasted_iota(I32, (16, 128), 1)
    a16 = jnp.zeros((16, 128), I32)
    for s in range(16):
        a16 = jnp.where(sub16 == s, assign_ref[s], a16)
    cnt = [jnp.float32(0.0)] * 4
    for s in range(16):
        for i in range(4):
            cnt[i] = cnt[i] + jnp.where(assign_ref[s] == i, 1.0, 0.0)
    sub8 = lax.broadcasted_iota(I32, (8, 128), 0)
    counts = jnp.zeros((8, 128), F32)
    for i in range(4):
        counts = jnp.where(lax.rem(sub8, 4) == i, cnt[i], counts)
    sel = jnp.zeros((8, 128), F32)
    lane8 = lax.broadcasted_iota(I32, (8, 128), 1)
    for tok in range(2):
        for s in range(16):
            hit = (lane8 == tok * 16 + s) & (sub8 == tok * 4 + assign_ref[s])
            sel = jnp.where(hit, 1.0, sel)
    oh8[...] = jnp.concatenate([sel, jnp.zeros((8, 128), F32)], axis=0).astype(BF16)

    def swap(b):
        return lax.rem(b, 4) * 4 + b // 4

    a16w = jnp.concatenate([a16, a16], axis=1)
    col16 = lax.broadcasted_iota(I32, (16, 256), 1)
    for tok in range(2):
        for ab in range(2):
            for half in range(2):

                def fill(b, _, tok=tok, ab=ab, half=half):
                    blk = b if tok == ab else swap(b)
                    target = a16w + (blk * 16 + half * 8 + tok * 4)
                    onehot[ab, half, pl.ds(pl.multiple_of(tok * 256 + b * 16, 16), 16), :] = jnp.where(
                        col16 == target, 1.0, 0.0
                    ).astype(BF16)
                    return 0

                lax.fori_loop(0, 16, fill, 0)

    for g in img_g:
        g.second(1)

    for s in z_order:
        peer = wrap(z - s, 8)
        rcopy(rc.at[peer], rc.at[peer], z_send.at[s], z_recv.at[s], z_peer(s)).wait_recv()
        rcopy(seedg.at[peer], seedg.at[peer], s_send.at[s], s_recv.at[s], z_peer(s)).wait_recv()
    ld_cot.wait()
    for k in range(8):
        for tok in range(2):
            pk32[tok * 16 + 2 * k : tok * 16 + 2 * k + 2, :] = rc[k, tok].astype(F32)
    for g in img_g:
        g.end(1)
        g.first(2)
    for j in range(NCH):
        for ab in range(2):
            cg[j, ab, p2[ab], p1[ab]] = pk32[ab * 16 : (ab + 1) * 16, j * W : (j + 1) * W].astype(BF16)
        cot_g[j].first(1)

    for k in range(8):
        for e in range(2):
            s = 2 * k + e
            pos = lax.broadcasted_iota(I32, (1, 3072), 1)
            row = seedg[k, e : e + 1, 0:1] * 1013904223
            base[s : s + 1, :] = (pos + c * 3072) * 1664525 + row

    g0 = gain_ref[...]
    g_hi = g0.astype(BF16)
    g_mid = (g0 - g_hi.astype(F32)).astype(BF16)
    g_lo = (g0 - g_hi.astype(F32) - g_mid.astype(F32)).astype(BF16)
    sub_g = lax.broadcasted_iota(I32, (16, 3072), 0)
    scl[512:528, :] = jnp.where(
        sub_g == 0,
        g_hi.astype(F32),
        jnp.where(sub_g == 1, g_mid.astype(F32), jnp.where(sub_g == 2, g_lo.astype(F32), 0.0)),
    ).astype(BF16)

    for g in img_g:
        g.second(2)
    cot_g[0].second(1)
    cot_g[1].second(1)
    cot_g[0].end(1)
    cot_g[0].first(2)
    for ch in range(2):
        img_g[ch].end(2)
        for ab in range(2):
            for half in range(2):
                lo = ab * 1536 + half * 768 + ch * 384
                noisy[:, lo : lo + 384] = dot_nn(onehot[ab, half], imgg[ch, ab].reshape(256, 384))

    def pump(k):
        if 0 <= k < NCH:
            cot_g[k].second(1)
        if 0 <= k - 1 < NCH:
            cot_g[k - 1].end(1)
            cot_g[k - 1].first(2)
        if 0 <= k - 2 < NCH:
            cot_g[k - 2].second(2)

    def token_of(tok, b):
        rr = b if tok == 0 else swap(b)
        return rr * 16 + z * 2 + tok

    def noise_block(tok, b, carry):
        tot, m2 = carry
        rows = pl.ds(pl.multiple_of(tok * 256 + b * 16, 16), 16)
        mixed = base[...] + token_of(tok, b) * D * 1664525
        mixed = mixed ^ (mixed >> 13)
        mixed = mixed * 1274126177
        mixed = mixed ^ (mixed >> 16)
        field = (mixed & 65535).astype(F32) - 32767.5
        v = noisy[rows, :] + field * (noise_scale / 18918.0)
        noisy[rows, :] = v
        s1 = jnp.sum(v, axis=1, keepdims=True)
        dev = v - s1 * (1.0 / 3072.0)
        s2 = jnp.sum(dev * dev, axis=1, keepdims=True)
        hit = lane == tok * 16 + b
        return jnp.where(hit, s1, tot), jnp.where(hit, s2, m2)

    carry = (jnp.zeros((16, 128), F32), jnp.zeros((16, 128), F32))
    carry = lax.fori_loop(0, 8, lambda b, cr: noise_block(0, b, cr), carry)
    pump(2)
    carry = lax.fori_loop(8, 16, lambda b, cr: noise_block(0, b, cr), carry)
    carry = lax.fori_loop(0, 8, lambda b, cr: noise_block(1, b, cr), carry)
    pump(3)
    carry = lax.fori_loop(8, 16, lambda b, cr: noise_block(1, b, cr), carry)
    stat[0], stat[1] = carry
    cp_stat = rcopy(stat, stat_in, k_send.at[0], k_recv.at[0], other)
    cp_stat.start()
    pump(4)
    cp_stat.wait_recv()
    mean_a, mean_b = stat[0] * (1.0 / 3072.0), stat_in[0] * (1.0 / 3072.0)
    gap = mean_a - mean_b
    var = (stat[1] + stat_in[1] + gap * gap * 1536.0) * (1.0 / D)
    mi[0] = (mean_a + mean_b) * 0.5
    mi[1] = lax.rsqrt(var + 1e-06)

    def pick(arr, idx):
        return jnp.sum(jnp.where(lane == idx, arr, 0.0), axis=1, keepdims=True)

    def norm_block(k, _):
        rows = pl.ds(pl.multiple_of(k * 16, 16), 16)
        normed = (noisy[rows, :] - pick(mi[0], k)) * pick(mi[1], k)
        scl[rows, :] = (normed * gain_ref[...]).astype(BF16)
        return 0

    lax.fori_loop(0, 32, norm_block, 0)
    pump(5)
    ld_up.wait()
    ld_dn.wait()

    def pre_cols(n):
        res = dot_nn(scl[...], up_v[:, n * 256 : (n + 1) * 256])
        pre[0, :, n * 256 : (n + 1) * 256] = res[0:256]
        pre[1, :, n * 256 : (n + 1) * 256] = res[256:512]
        ugp[:, n * 256 : (n + 1) * 256] = res[512:528]

    pre_cols(0)
    pump(6)
    pre_cols(1)
    pump(7)
    pre_cols(2)
    cp_pre = rcopy(pre.at[1 - c], pre_in, k_send.at[1], k_recv.at[1], other)
    cp_pre.start()
    cp_ug = rcopy(ugp, ug_in, k_send.at[2], k_recv.at[2], other)
    cp_ug.start()

    def back_chunk(j, ab):
        dim = cg[j, ab].reshape(256, W)
        res = dot_nt(dim, dn_v[:, j * W : (j + 1) * W])
        if j == 0:
            bk[ab] = res
        else:
            bk[ab] = bk[ab] + res

    for j in range(NCH - 1):
        cot_g[j].end(2)
        for ab in range(2):
            back_chunk(j, ab)
        if j == 0:
            cp_pre.wait_recv()
            cp_ug.wait_recv()
        if j == 1:

            def slope_block(k, _):
                rows = pl.ds(pl.multiple_of(k * 16, 16), 16)
                p = pre[c, rows, :] + pre_in[rows, :]
                pre_in[rows, :] = p
                slope[rows, :] = gelu_slope(p)
                return 0

            lax.fori_loop(0, 16, slope_block, 0)
        if j == 2:
            def wt_block(b, _):
                rr = jnp.where(c == 0, b, swap(b))
                inv = pick(mi[1], c * 16 + b)
                wt[pl.ds(pl.multiple_of(b * 16, 16), 16), :] = jnp.where(
                    lane == rr * 8 + c * 4 + a16, inv, 0.0
                )
                return 0

            lax.fori_loop(0, 16, wt_block, 0)
            full = wt[...].T
            hi = full.astype(BF16)
            mid = (full - hi.astype(F32)).astype(BF16)
            lo = (full - hi.astype(F32) - mid.astype(F32)).astype(BF16)
            wm[0:128] = hi
            wm[128:256] = mid
            wm[256:384] = lo
    cot_g[NCH - 1].end(2)
    last = NCH - 1
    for flip in (1, 0):
        ab = (c + flip) % 2
        dim = cg[last, ab].reshape(256, W)
        bk[ab] = bk[ab] + dot_nt(dim, dn_v[:, last * W :])
        if flip == 1:
            cp_bk = rcopy(bk.at[1 - c], bk_in, k_send.at[3], k_recv.at[3], other)
            cp_bk.start()
    ug = (ugp[0:1] + ugp[1:2] + ugp[2:3]) + (ug_in[0:1] + ug_in[1:2] + ug_in[2:3])
    cp_bk.wait_recv()

    def hidden_block(b, carry):
        gs, gd = carry
        rows = pl.ds(pl.multiple_of(b * 16, 16), 16)
        hg = ((bk[c, rows, :] + bk_in[rows, :]) * slope[rows, :]).astype(BF16)
        scl[rows, 0:768] = hg
        hf = hg.astype(F32)
        s1 = jnp.sum(hf * ug, axis=1, keepdims=True)
        s2 = jnp.sum(hf * pre_in[rows, :], axis=1, keepdims=True)
        hit = lane == c * 16 + b
        return jnp.where(hit, s1, gs), jnp.where(hit, s2, gd)

    zero = jnp.zeros((16, 128), F32)
    gst[0], gst[1] = lax.fori_loop(0, 16, hidden_block, (zero, zero))
    cp_gst = rcopy(gst, gst_in, k_send.at[4], k_recv.at[4], other)
    cp_gst.start()
    wsum = dot_nn(wm[...], scl[0:256, 0:768])
    wsum = wsum[0:128] + wsum[128:256] + wsum[256:384]
    w_hi = wsum.astype(BF16)
    wx[0:128] = w_hi
    wx[128:256] = (wsum - w_hi.astype(F32)).astype(BF16)
    cp_wx = rcopy(wx, wx_in, k_send.at[5], k_recv.at[5], other)
    cp_wx.start()

    cp_gst.wait_recv()
    gx[...] = gst[...] + gst_in[...]

    def g_copy(axis, src, dst, step):
        k = axis * 3 + step - 1
        return rcopy(src, dst.at[step - 1], g_send.at[k], g_recv.at[k], row_peer(0, axis + 1, step))

    for step in (1, 2, 3):
        g_copy(0, gx, gx_in, step).start()

    cp_wx.wait_recv()
    wall[...] = (wx[...].astype(F32) + wx_in[...].astype(F32)).astype(BF16)

    def r1_copy(ab, step):
        k = ab * 6 + step - 1
        return rcopy(
            rs.at[ab, wrap(p1[ab] + step, 4)], rr1.at[ab, step - 1], r_send.at[k], r_recv.at[k], row_peer(ab, 1, step)
        )

    def r2_copy(ab, step):
        k = ab * 6 + 3 + step - 1
        return rcopy(
            ss.at[ab, wrap(p2[ab] + step, 4)], rr2.at[ab, step - 1], r_send.at[k], r_recv.at[k], row_peer(ab, 2, step)
        )

    for ab in range(2):
        for half in range(2):
            q = ab * 2 + half
            o = dot_nt(wall[...], up_v[q * 768 : (q + 1) * 768, :])
            o_s[ab, half] = o[0:128] + o[128:256]

        def pack(k, _, ab=ab):
            rows = pl.ds(pl.multiple_of(k * 8, 8), 8)
            both = jnp.concatenate([o_s[ab, 0, rows, :], o_s[ab, 1, rows, :]], axis=0)
            ky, kx = k // 4, lax.rem(k, 4)
            rs[ab, kx if ab == 0 else ky, ky if ab == 0 else kx] = both.astype(BF16)
            return 0

        lax.fori_loop(0, 16, pack, 0)
        for step in (1, 2, 3):
            r1_copy(ab, step).start()
        if ab == 0:
            for step in (1, 2, 3):
                g_copy(0, gx, gx_in, step).wait_recv()
            gy[...] = gx[...] + gx_in[0] + gx_in[1] + gx_in[2]
            for step in (1, 2, 3):
                g_copy(1, gy, gy_in, step).start()

    for step in (1, 2, 3):
        g_copy(1, gy, gy_in, step).wait_recv()
    gtot = (gy[...] + gy_in[0] + gy_in[1] + gy_in[2]) * (1.0 / D)
    own_b = (y * 4 + x, x * 4 + y)
    for tok in range(2):
        k = tok * 16 + own_b[tok]
        rows = pl.ds(pl.multiple_of(tok * 256 + own_b[tok] * 16, 16), 16)
        inv = pick(mi[1], k)
        normed = (noisy[rows, :] - pick(mi[0], k)) * inv
        v = inv * (pick(gtot[0], k) + normed * pick(gtot[1], k))
        pk32[tok * 16 : tok * 16 + 16, :] = pk32[tok * 16 : tok * 16 + 16, :] - v
    rest = pk32[...]
    t1 = rest.astype(BF16)
    t2 = (rest - t1.astype(F32)).astype(BF16)
    t3 = (rest - t1.astype(F32) - t2.astype(F32)).astype(BF16)
    pick8 = oh8[:, 0:32]
    rest8 = (dot_nn(pick8, t1) + dot_nn(pick8, t2) + dot_nn(pick8, t3))[0:8]

    for ab in range(2):
        for step in (1, 2, 3):
            r1_copy(ab, 4 - step).wait_recv()

        def add1(k, _, ab=ab):
            kr = (k * 4 + p1[0]) if ab == 0 else (p1[1] * 4 + k)
            rows = pl.ds(pl.multiple_of(kr * 8, 8), 8)
            both = jnp.concatenate([o_s[ab, 0, rows, :], o_s[ab, 1, rows, :]], axis=0)
            for n in range(3):
                both = both + rr1[ab, n, k].astype(F32)
            ss[ab, k] = both.astype(BF16)
            return 0

        lax.fori_loop(0, 4, add1, 0)
        for step in (1, 2, 3):
            r2_copy(ab, step).start()

    cnt8 = counts[:, 0:1]
    for ab in range(2):
        for step in (1, 2, 3):
            r2_copy(ab, step).wait_recv()
        tot = ss[ab, p2[ab]].astype(F32)
        for n in range(3):
            tot = tot + rr2[ab, n].astype(F32)
        for half in range(2):
            lo = ab * 1536 + half * 768
            g8 = tot[half * 8 : half * 8 + 8] * gain_ref[:, lo : lo + 768]
            fin = (g8 + rest8[:, lo : lo + 768]) / cnt8
            out_v[2 * z, :, lo : lo + 768] = fin[0:4]
            out_v[2 * z + 1, :, lo : lo + 768] = fin[4:8]

    def o_copy(n, way):
        step = 1 if way == 0 else -1
        src = wrap(z - step * (n - 1) + 8, 8)
        k = (n - 1) * 2 + way
        if n < 4:
            ref = out_v.at[pl.ds(2 * src, 2)]
        else:
            ref = out_v.at[pl.ds(2 * src + way, 1)]
        return rcopy(ref, ref, o_send.at[k], o_recv.at[k], z_peer(step))

    for n in (1, 2, 3, 4):
        for way in (0, 1):
            if n > 1:
                o_copy(n - 1, way).wait_recv()
            o_copy(n, way).start()
    for way in (0, 1):
        o_copy(4, way).wait_recv()
    st_out = pltpu.make_async_copy(out_v, out_hbm, load_sem.at[4])
    st_out.start()
    for cp in sends:
        cp.wait_send()
    for g in img_g + cot_g:
        g.drain()
    for cp in (cp_stat, cp_pre, cp_ug, cp_bk, cp_gst, cp_wx):
        cp.wait_send()
    for axis in range(2):
        for step in (1, 2, 3):
            g_copy(axis, gx, gx_in, step).wait_send()
    for ab in range(2):
        for step in (1, 2, 3):
            r1_copy(ab, step).wait_send()
            r2_copy(ab, step).wait_send()
    for n in (1, 2, 3, 4):
        for way in (0, 1):
            o_copy(n, way).wait_send()
    st_out.wait()


def body(images, gain, up_weight, down_weight, cotangent, seeds, assign):
    W = 3072 // NCH
    vm, dma = pltpu.VMEM, pltpu.SemaphoreType.DMA
    anyspace = pl.BlockSpec(memory_space=pl.ANY)
    return pl.pallas_call(
        kernel,
        out_shape=jax.ShapeDtypeStruct((16, 4, 3072), F32),
        in_specs=[
            anyspace,
            pl.BlockSpec(memory_space=pltpu.VMEM),
            anyspace,
            anyspace,
            anyspace,
            pl.BlockSpec(memory_space=pltpu.SMEM),
            pl.BlockSpec(memory_space=pltpu.SMEM),
        ],
        out_specs=anyspace,
        scratch_shapes=[
            vm((3072, 768), BF16),
            vm((768, 3072), BF16),
            vm((2, 4, 3072), BF16),
            vm((16, 1536), F32),
            vm((2, 2, 4, 4, 16, 384), BF16),
            vm((8, 2, 2, 3072), BF16),
            vm((8, 8, 128), I32),
            vm((32, 3072), F32),
            vm((NCH, 2, 4, 4, 16, W), BF16),
            vm((2, 2, 512, 256), BF16),
            vm((16, 3072), I32),
            vm((512, 3072), F32),
            vm((528, 3072), BF16),
            vm((2, 256, 768), F32),
            vm((256, 768), F32),
            vm((16, 768), F32),
            vm((16, 768), F32),
            vm((256, 768), F32),
            vm((2, 256, 768), F32),
            vm((256, 768), F32),
            vm((2, 16, 128), F32),
            vm((2, 16, 128), F32),
            vm((2, 16, 128), F32),
            vm((2, 16, 128), F32),
            vm((2, 16, 128), F32),
            vm((256, 128), F32),
            vm((384, 256), BF16),
            vm((256, 768), BF16),
            vm((256, 768), BF16),
            vm((256, 768), BF16),
            vm((2, 2, 128, 768), F32),
            vm((2, 4, 4, 16, 768), BF16),
            vm((2, 3, 4, 16, 768), BF16),
            vm((2, 4, 16, 768), BF16),
            vm((2, 3, 16, 768), BF16),
            vm((2, 16, 128), F32),
            vm((3, 2, 16, 128), F32),
            vm((2, 16, 128), F32),
            vm((3, 2, 16, 128), F32),
            vm((16, 128), BF16),
            vm((16, 4, 3072), F32),
            dma((5,)),
            dma((8,)), dma((8,)),
            dma((8,)), dma((8,)),
            dma((2, 12)), dma((2, 12)),
            dma((NCH, 12)), dma((NCH, 12)),
            dma((6,)), dma((6,)),
            dma((12,)), dma((12,)),
            dma((6,)), dma((6,)),
            dma((8,)), dma((8,)),
        ],
        compiler_params=pltpu.CompilerParams(
            collective_id=0, has_side_effects=True, vmem_limit_bytes=56 * 1024 * 1024
        ),
        cost_estimate=pl.CostEstimate(flops=8 * 10**9, bytes_accessed=12 * 10**6, transcendentals=200000),
    )(images, gain.reshape(1, -1), up_weight, down_weight, cotangent, seeds, assign.reshape(-1))


def solution(mesh):
    placed = (
        P("row", None, "col"),
        P("col"),
        P("col", "row"),
        P("row", "col"),
        P("row", "noise", "col"),
        P("noise"),
        P(),
    )
    return jax.shard_map(
        body, mesh=mesh, in_specs=placed, out_specs=P("row", None, "col"), check_vma=False
    )
```

time: 362 us -> 102 us (0.28)
  waiting for transfers between devices: 290 us -> 0 us
  Pallas kernels: 0 us -> 99.2 us
  matrix products: 26.6 us -> 0 us
  local copies, waits for them, and re-layouts: 17.2 us -> 2.07 us
  between operations: 13.2 us -> 0.01 us
  blocking collectives: 8.21 us -> 0 us
  other arithmetic: 5.16 us -> 0 us
    psum x2 -> x0, waiting for transfers between devices: 107 us -> none  [the longest x1 73.9 us: body(): totals = lax.psum(partial_totals, 'noise')]
    pallas_call x0 -> x1, Pallas kernels: none -> 99.2 us  [body(): pl.pallas_call(kernel, out_shape=jax.ShapeDtypeStruct((16, 4, 3072), F32)...]
    all_gather x2 -> x0, waiting for transfers between devices: 94.7 us -> none  [the longest x1 54.9 us: body(): lax.all_gather(scaled, 'row', axis=0, tiled=True)]
    reduce_scatter x1 -> x0, waiting for transfers between devices: 87.6 us -> none  [body(): lax.psum_scatter(jnp.einsum('th,dh->td', hidden_grad, up_weight, preferre...]
    dot_general x5 -> x0, matrix products: 26.6 us -> none  [the longest x1 9.19 us: body(): jnp.einsum('th,dh->td', hidden_grad, up_weight, preferred_element_type=jn...]
    reshape x3 -> x0, local copies, waits for them, and re-layouts: 16.3 us -> none  [the longest x1 7.54 us: body(): full_scaled = gathered[0].reshape(row_count, width_local)]
    psum x3 -> x0, blocking collectives: 8.21 us -> none  [the longest x1 3.29 us: body(): lax.psum((jnp.sum(normed_grad, axis=-1), jnp.sum(normed_grad * normed, ax...]
  transfers between devices with their start and end apart: 5 -> 0, of which waited for: 5 -> 0; matrix products, arithmetic and copies ran while one was open for 4% -> 0% of each run, Pallas kernels for 0% -> 0%
where the time goes in v2:
time: 102 us; the launch traced here: 101 us
  Pallas kernels  99.2 us (97%)
  local copies, waits for them, and re-layouts  2.07 us (2%)
    pallas_call x1, Pallas kernels, body(): pl.pallas_call(kernel, out_shape=jax.ShapeDtypeStruct((16, 4, 3072), F32)...  99.2 us
    unnamed x1, local copies, waits for them, and re-layouts  2.07 us

profile of v2, /device:TPU:32, one launch (start us, length us, event | category | flops | bytes accessed | tf_op | source)
XLA Modules:
  0.0 101.3 jit_solution(17621852254707474300)
XLA Ops:
  0.0 99.2 %shard_map.73 = f32[16,4,3072]{2,1,0:T(4,128)} custom-call(bf16[16,4,3072]{2,1,0:T(4,128)(2,1)} %img_hbm.1, f32[1,3072]{1,0:T(1,128)} %bitcast.2, bf16[3072,768]{1,0:T(8,128)(2,1)} %up_hbm.1, bf16[768,3072]{1,0:T(8,128)(2,1)} %dn_hbm.1, bf16[16,2,3072]{2,1,0:T(2,128)(2,1)} %cot_hbm.1, s32[2]{0:T(128)} %seeds_ref.1, s32[16]{0:T(128)} %bitcast.3), custom_call_target="tpu_custom_call" | custom-call | flops 8000000000 | bytes 12000000 | tf_op jit(solution)/shard_map/pallas_call | solution.py:553
  99.2 2.1 %copy.9 = f32[16,4,3072]{2,1,0:T(4,128)} copy(f32[16,4,3072]{2,1,0:T(4,128)} %shard_map.73) | data formatting | bytes 1572864

commit v3 on v2

v3 whole, which is shorter than its diff:
```python
import functools
import math

import jax
import jax.numpy as jnp
from jax import lax
from jax.experimental import pallas as pl
from jax.experimental.pallas import tpu as pltpu
from jax.sharding import PartitionSpec as P

D = 6144
NCH = 4
noise_scale = 0.6
gelu_coef = 0.044715
root_term = math.sqrt(2.0 / math.pi)
MESH = pl.DeviceIdType.MESH
F32 = jnp.float32
BF16 = jnp.bfloat16
I32 = jnp.int32


def gelu_slope(preact):
    inner = root_term * (preact + gelu_coef * preact * preact * preact)
    tanh_val = jnp.tanh(inner)
    return 0.5 * (1.0 + tanh_val) + 0.5 * preact * (1.0 - tanh_val * tanh_val) * root_term * (
        1.0 + 3.0 * gelu_coef * preact * preact
    )


def dot_nt(a, b):
    return lax.dot_general(a, b, (((1,), (1,)), ((), ())), preferred_element_type=F32)


def dot_nn(a, b):
    return lax.dot_general(a, b, (((1,), (0,)), ((), ())), preferred_element_type=F32)


class Copy:
    def __init__(self, live, src, dst, ssem, rsem, dev):
        self.live, self.got = live, False
        self.make = lambda: pltpu.make_async_remote_copy(
            src_ref=src, dst_ref=dst, send_sem=ssem, recv_sem=rsem, device_id=dev, device_id_type=MESH
        )

    def start(self):
        self.made = self.make()
        self.made.start()
        self.live.append(self)

    def wait_recv(self):
        self.made.wait_recv()
        self.got = True

    def wait_send(self):
        self.made.wait_send()


def wrap(i, n):
    return lax.rem(i + n, n)


def kernel(
    img_hbm, gain_ref, up_hbm, dn_hbm, cot_hbm, seeds_ref, assign_ref, outa_hbm, outb_hbm,
    up_v, dn_v, img_own, pk16, imgg, rc, seedg, pk32, cg, onehot, base, noisy, scl,
    pre, pre_in, ugp, ug_in, slope, bk, bk_in, stat, stat_in, mi, gst, gst_in, wt, wm, wx, wx_in, wall,
    o_s, rs, rr, gx, gx_in, gy, gy_in, oh8, ea_own, la_own,
    load_sem, z_send, z_recv, s_send, s_recv, i_send, i_recv, c_send, c_recv, k_send, k_recv,
    r_send, r_recv, g_send, g_recv, e_send, e_recv, l_send, l_recv,
):
    W = 3072 // NCH
    z = lax.axis_index("noise")
    r = lax.axis_index("row")
    c = lax.axis_index("col")
    y, x = r // 4, lax.rem(r, 4)
    p1 = (x, y)
    p2 = (y, x)

    def row_peer(ab, phase, step):
        along_x = (ab == 0) == (phase == 1)
        if along_x:
            return {"row": y * 4 + wrap(x + step, 4)}
        return {"row": wrap(y + step, 4) * 4 + x}

    def z_peer(step):
        return {"noise": wrap(z + step, 8)}

    other = {"col": 1 - c}

    live = []

    def rcopy(src, dst, ssem, rsem, dev):
        return Copy(live, src, dst, ssem, rsem, dev)

    ld_img = pltpu.make_async_copy(img_hbm.at[pl.ds(2 * z, 2)], img_own, load_sem.at[0])
    ld_img.start()
    ld_cot = pltpu.make_async_copy(cot_hbm.at[pl.ds(2 * z, 2)], rc.at[z], load_sem.at[1])
    ld_cot.start()
    ld_up = pltpu.make_async_copy(up_hbm, up_v, load_sem.at[2])
    ld_up.start()
    ld_dn = pltpu.make_async_copy(dn_hbm, dn_v, load_sem.at[3])
    ld_dn.start()

    barrier = pltpu.get_barrier_semaphore()
    for dev in (
        [z_peer(s) for s in range(1, 8)]
        + [{"row": wrap(y + k // 4, 4) * 4 + wrap(x + k % 4, 4)} for k in range(1, 16)]
        + [other]
    ):
        pl.semaphore_signal(barrier, inc=1, device_id=dev, device_id_type=MESH)

    seedg[z] = jnp.where(
        lax.broadcasted_iota(I32, (8, 128), 0) == 0, seeds_ref[0], seeds_ref[1]
    )
    ld_img.wait()
    for tok in range(2):
        v = img_own[tok].astype(F32)
        for q in range(4):
            ab, half = q // 2, q % 2
            pk16[half * 8 + tok * 4 : half * 8 + tok * 4 + 4, ab * 768 : (ab + 1) * 768] = v[
                :, q * 768 : (q + 1) * 768
            ]
    for ch in range(2):
        for ab in range(2):
            lo = ab * 768 + ch * 384
            imgg[ch, ab, p2[ab], p1[ab]] = pk16[:, lo : lo + 384].astype(BF16)
    pl.semaphore_wait(barrier, 23)

    z_order = (1, 7, 2, 6, 3, 5, 4)
    z_cot, z_seed = {}, {}
    for s in z_order:
        peer = wrap(z + s, 8)
        z_cot[s] = rcopy(cot_hbm.at[pl.ds(2 * peer, 2)], rc.at[z], z_send.at[s], z_recv.at[s], z_peer(s))
        z_seed[s] = rcopy(seedg.at[z], seedg.at[z], s_send.at[s], s_recv.at[s], z_peer(s))
        z_cot[s].start()
        z_seed[s].start()

    class Gather:
        def __init__(self, buf, ssem, rsem):
            self.copies = {}
            for ab in range(2):
                for phase in (1, 2):
                    own = buf.at[ab, p2[ab], p1[ab]] if phase == 1 else buf.at[ab, p2[ab]]
                    for step in (1, 3, 2):
                        k = (ab * 2 + phase - 1) * 3 + step - 1
                        self.copies[ab, phase, step] = rcopy(
                            own, own, ssem.at[k], rsem.at[k], row_peer(ab, phase, step)
                        )

        def start(self, phase):
            for step in (1, 3, 2):
                for ab in range(2):
                    self.copies[ab, phase, step].start()

        def wait(self, phase):
            for step in (1, 3, 2):
                for ab in range(2):
                    self.copies[ab, phase, step].wait_recv()

    img_g = [Gather(imgg.at[ch], i_send.at[ch], i_recv.at[ch]) for ch in range(2)]
    cot_g = [Gather(cg.at[j], c_send.at[j], c_recv.at[j]) for j in range(NCH)]

    for g in img_g:
        g.start(1)

    sub16 = lax.broadcasted_iota(I32, (16, 128), 0)
    lane = lax.broadcasted_iota(I32, (16, 128), 1)
    a16 = jnp.zeros((16, 128), I32)
    for s in range(16):
        a16 = jnp.where(sub16 == s, assign_ref[s], a16)
    cnt = [jnp.float32(0.0)] * 4
    for s in range(16):
        for i in range(4):
            cnt[i] = cnt[i] + jnp.where(assign_ref[s] == i, 1.0, 0.0)
    sub8 = lax.broadcasted_iota(I32, (8, 128), 0)
    counts = jnp.zeros((8, 128), F32)
    for i in range(4):
        counts = jnp.where(lax.rem(sub8, 4) == i, cnt[i], counts)
    cnt8 = counts[:, 0:1]
    sel = jnp.zeros((8, 128), F32)
    lane8 = lax.broadcasted_iota(I32, (8, 128), 1)
    for tok in range(2):
        for s in range(16):
            hit = (lane8 == tok * 16 + s) & (sub8 == tok * 4 + assign_ref[s])
            sel = jnp.where(hit, 1.0, sel)
    oh8[...] = jnp.concatenate([sel, jnp.zeros((8, 128), F32)], axis=0).astype(BF16)

    def swap(b):
        return lax.rem(b, 4) * 4 + b // 4

    a16w = jnp.concatenate([a16, a16], axis=1)
    col16 = lax.broadcasted_iota(I32, (16, 256), 1)
    for tok in range(2):
        for ab in range(2):
            for half in range(2):

                def fill(b, _, tok=tok, ab=ab, half=half):
                    blk = b if tok == ab else swap(b)
                    target = a16w + (blk * 16 + half * 8 + tok * 4)
                    onehot[ab, half, pl.ds(pl.multiple_of(tok * 256 + b * 16, 16), 16), :] = jnp.where(
                        col16 == target, 1.0, 0.0
                    ).astype(BF16)
                    return 0

                lax.fori_loop(0, 16, fill, 0)

    for g in img_g:
        g.wait(1)
        g.start(2)

    for s in z_order:
        z_cot[s].wait_recv()
        z_seed[s].wait_recv()
    ld_cot.wait()
    for k in range(8):
        for tok in range(2):
            pk32[tok * 16 + 2 * k : tok * 16 + 2 * k + 2, :] = rc[k, tok].astype(F32)
    for j in range(NCH):
        for ab in range(2):
            cg[j, ab, p2[ab], p1[ab]] = pk32[ab * 16 : (ab + 1) * 16, j * W : (j + 1) * W].astype(BF16)
        cot_g[j].start(1)
    early8 = dot_nn(oh8[:, 0:32], pk32[...].astype(BF16))[0:8] / cnt8
    ea_own[0], ea_own[1] = early8[0:4], early8[4:8]
    ld_ea = pltpu.make_async_copy(ea_own, outa_hbm.at[pl.ds(2 * z, 2)], load_sem.at[4])
    ld_ea.start()
    ea = {s: rcopy(ea_own, outa_hbm.at[pl.ds(2 * z, 2)], e_send.at[s], e_recv.at[s], z_peer(s)) for s in z_order}
    for s in z_order:
        ea[s].start()

    for k in range(8):
        for e in range(2):
            s = 2 * k + e
            pos = lax.broadcasted_iota(I32, (1, 3072), 1)
            row = seedg[k, e : e + 1, 0:1] * 1013904223
            base[s : s + 1, :] = (pos + c * 3072) * 1664525 + row

    g0 = gain_ref[...]
    g_hi = g0.astype(BF16)
    g_mid = (g0 - g_hi.astype(F32)).astype(BF16)
    g_lo = (g0 - g_hi.astype(F32) - g_mid.astype(F32)).astype(BF16)
    sub_g = lax.broadcasted_iota(I32, (16, 3072), 0)
    scl[512:528, :] = jnp.where(
        sub_g == 0,
        g_hi.astype(F32),
        jnp.where(sub_g == 1, g_mid.astype(F32), jnp.where(sub_g == 2, g_lo.astype(F32), 0.0)),
    ).astype(BF16)

    for ch in range(2):
        img_g[ch].wait(2)
        for ab in range(2):
            for half in range(2):
                lo = ab * 1536 + half * 768 + ch * 384
                noisy[:, lo : lo + 384] = dot_nn(onehot[ab, half], imgg[ch, ab].reshape(256, 384))

    def pump(k):
        cot_g[k].wait(1)
        cot_g[k].start(2)

    pump(0)

    def token_of(tok, b):
        rr = b if tok == 0 else swap(b)
        return rr * 16 + z * 2 + tok

    def noise_block(tok, b, carry):
        tot, m2 = carry
        rows = pl.ds(pl.multiple_of(tok * 256 + b * 16, 16), 16)
        mixed = base[...] + token_of(tok, b) * D * 1664525
        mixed = mixed ^ (mixed >> 13)
        mixed = mixed * 1274126177
        mixed = mixed ^ (mixed >> 16)
        field = (mixed & 65535).astype(F32) - 32767.5
        v = noisy[rows, :] + field * (noise_scale / 18918.0)
        noisy[rows, :] = v
        s1 = jnp.sum(v, axis=1, keepdims=True)
        dev = v - s1 * (1.0 / 3072.0)
        s2 = jnp.sum(dev * dev, axis=1, keepdims=True)
        hit = lane == tok * 16 + b
        return jnp.where(hit, s1, tot), jnp.where(hit, s2, m2)

    carry = (jnp.zeros((16, 128), F32), jnp.zeros((16, 128), F32))
    def noise_blocks(tok, first, carry):
        def four(k, cr):
            for u in range(4):
                cr = noise_block(tok, first + k * 4 + u, cr)
            return cr

        return lax.fori_loop(0, 2, four, carry)

    carry = noise_blocks(0, 0, carry)
    pump(1)
    carry = noise_blocks(0, 8, carry)
    pump(2)
    carry = noise_blocks(1, 0, carry)
    pump(3)
    carry = noise_blocks(1, 8, carry)
    stat[0], stat[1] = carry
    cp_stat = rcopy(stat, stat_in, k_send.at[0], k_recv.at[0], other)
    cp_stat.start()
    cp_stat.wait_recv()
    mean_a, mean_b = stat[0] * (1.0 / 3072.0), stat_in[0] * (1.0 / 3072.0)
    gap = mean_a - mean_b
    var = (stat[1] + stat_in[1] + gap * gap * 1536.0) * (1.0 / D)
    mi[0] = (mean_a + mean_b) * 0.5
    mi[1] = lax.rsqrt(var + 1e-06)

    def pick(arr, idx):
        return jnp.sum(jnp.where(lane == idx, arr, 0.0), axis=1, keepdims=True)

    def norm_blocks(k4, _):
        for u in range(4):
            k = k4 * 4 + u
            rows = pl.ds(pl.multiple_of(k * 16, 16), 16)
            normed = (noisy[rows, :] - pick(mi[0], k)) * pick(mi[1], k)
            scl[rows, :] = (normed * gain_ref[...]).astype(BF16)
        return 0

    lax.fori_loop(0, 8, norm_blocks, 0)
    ld_up.wait()
    ld_dn.wait()

    def pre_cols(n):
        res = dot_nn(scl[...], up_v[:, n * 256 : (n + 1) * 256])
        pre[0, :, n * 256 : (n + 1) * 256] = res[0:256]
        pre[1, :, n * 256 : (n + 1) * 256] = res[256:512]
        ugp[:, n * 256 : (n + 1) * 256] = res[512:528]

    pre_cols(0)
    pre_cols(1)
    pre_cols(2)
    cp_pre = rcopy(pre.at[1 - c], pre_in, k_send.at[1], k_recv.at[1], other)
    cp_pre.start()
    cp_ug = rcopy(ugp, ug_in, k_send.at[2], k_recv.at[2], other)
    cp_ug.start()

    def back_chunk(j, ab):
        dim = cg[j, ab].reshape(256, W)
        res = dot_nt(dim, dn_v[:, j * W : (j + 1) * W])
        if j == 0:
            bk[ab] = res
        else:
            bk[ab] = bk[ab] + res

    for j in range(NCH - 1):
        cot_g[j].wait(2)
        for ab in range(2):
            back_chunk(j, ab)
        if j == 0:
            cp_pre.wait_recv()
            cp_ug.wait_recv()
        if j == 1:

            def slope_block(k, _):
                rows = pl.ds(pl.multiple_of(k * 16, 16), 16)
                p = pre[c, rows, :] + pre_in[rows, :]
                pre_in[rows, :] = p
                slope[rows, :] = gelu_slope(p)
                return 0

            lax.fori_loop(0, 16, slope_block, 0)
        if j == 2:
            def wt_block(b, _):
                rr = jnp.where(c == 0, b, swap(b))
                inv = pick(mi[1], c * 16 + b)
                wt[pl.ds(pl.multiple_of(b * 16, 16), 16), :] = jnp.where(
                    lane == rr * 8 + c * 4 + a16, inv, 0.0
                )
                return 0

            lax.fori_loop(0, 16, wt_block, 0)
            full = wt[...].T
            hi = full.astype(BF16)
            mid = (full - hi.astype(F32)).astype(BF16)
            lo = (full - hi.astype(F32) - mid.astype(F32)).astype(BF16)
            wm[0:128] = hi
            wm[128:256] = mid
            wm[256:384] = lo
    cot_g[NCH - 1].wait(2)
    last = NCH - 1
    for flip in (1, 0):
        ab = (c + flip) % 2
        dim = cg[last, ab].reshape(256, W)
        bk[ab] = bk[ab] + dot_nt(dim, dn_v[:, last * W :])
        if flip == 1:
            cp_bk = rcopy(bk.at[1 - c], bk_in, k_send.at[3], k_recv.at[3], other)
            cp_bk.start()
    ug = (ugp[0:1] + ugp[1:2] + ugp[2:3]) + (ug_in[0:1] + ug_in[1:2] + ug_in[2:3])
    cp_bk.wait_recv()

    def hidden_block(b, carry):
        gs, gd = carry
        rows = pl.ds(pl.multiple_of(b * 16, 16), 16)
        hg = ((bk[c, rows, :] + bk_in[rows, :]) * slope[rows, :]).astype(BF16)
        scl[rows, 0:768] = hg
        hf = hg.astype(F32)
        s1 = jnp.sum(hf * ug, axis=1, keepdims=True)
        s2 = jnp.sum(hf * pre_in[rows, :], axis=1, keepdims=True)
        hit = lane == c * 16 + b
        return jnp.where(hit, s1, gs), jnp.where(hit, s2, gd)

    def hidden_blocks(k, carry):
        for u in range(4):
            carry = hidden_block(k * 4 + u, carry)
        return carry

    zero = jnp.zeros((16, 128), F32)
    gst[0], gst[1] = lax.fori_loop(0, 4, hidden_blocks, (zero, zero))
    cp_gst = rcopy(gst, gst_in, k_send.at[4], k_recv.at[4], other)
    cp_gst.start()
    wsum = dot_nn(wm[...], scl[0:256, 0:768])
    wsum = wsum[0:128] + wsum[128:256] + wsum[256:384]
    w_hi = wsum.astype(BF16)
    wx[0:128] = w_hi
    wx[128:256] = (wsum - w_hi.astype(F32)).astype(BF16)
    cp_wx = rcopy(wx, wx_in, k_send.at[5], k_recv.at[5], other)
    cp_wx.start()

    cp_gst.wait_recv()
    gx[...] = gst[...] + gst_in[...]

    @functools.cache
    def g_copy(axis, step):
        src, dst = ((gx, gx_in), (gy, gy_in))[axis]
        k = axis * 3 + step - 1
        return rcopy(src, dst.at[step - 1], g_send.at[k], g_recv.at[k], row_peer(0, axis + 1, step))

    for step in (1, 2, 3):
        g_copy(0, step).start()

    cp_wx.wait_recv()
    wall[...] = (wx[...].astype(F32) + wx_in[...].astype(F32)).astype(BF16)

    far = sorted(range(1, 16), key=lambda k: min(k // 4, 4 - k // 4) + min(k % 4, 4 - k % 4))

    @functools.cache
    def r_copy(ab, k):
        peer = wrap(y + k // 4, 4) * 4 + wrap(x + k % 4, 4)
        return rcopy(rs.at[ab, peer], rr.at[ab, k], r_send.at[ab, k], r_recv.at[ab, k], {"row": peer})

    for ab in range(2):
        for half in range(2):
            q = ab * 2 + half
            o = dot_nt(wall[...], up_v[q * 768 : (q + 1) * 768, :])
            o_s[ab, half] = o[0:128] + o[128:256]

        def pack(k, _, ab=ab):
            rows = pl.ds(pl.multiple_of(k * 8, 8), 8)
            both = jnp.concatenate([o_s[ab, 0, rows, :], o_s[ab, 1, rows, :]], axis=0)
            rs[ab, k] = both.astype(BF16)
            return 0

        lax.fori_loop(0, 16, pack, 0)
        for k in far:
            r_copy(ab, k).start()
        if ab == 0:
            for step in (1, 2, 3):
                g_copy(0, step).wait_recv()
            gy[...] = gx[...] + gx_in[0] + gx_in[1] + gx_in[2]
            for step in (1, 2, 3):
                g_copy(1, step).start()

    for step in (1, 2, 3):
        g_copy(1, step).wait_recv()
    gtot = (gy[...] + gy_in[0] + gy_in[1] + gy_in[2]) * (1.0 / D)
    own_b = (y * 4 + x, x * 4 + y)
    for tok in range(2):
        k = tok * 16 + own_b[tok]
        rows = pl.ds(pl.multiple_of(tok * 256 + own_b[tok] * 16, 16), 16)
        inv = pick(mi[1], k)
        normed = (noisy[rows, :] - pick(mi[0], k)) * inv
        v = inv * (pick(gtot[0], k) + normed * pick(gtot[1], k))
        pk32[tok * 16 : tok * 16 + 16, :] = v
    rest = pk32[...]
    t1 = rest.astype(BF16)
    t2 = (rest - t1.astype(F32)).astype(BF16)
    t3 = (rest - t1.astype(F32) - t2.astype(F32)).astype(BF16)
    pick8 = oh8[:, 0:32]
    rest8 = (dot_nn(pick8, t1) + dot_nn(pick8, t2) + dot_nn(pick8, t3))[0:8]

    own_rows = pl.ds(pl.multiple_of(r * 8, 8), 8)
    for ab in range(2):
        tot = [o_s[ab, half, own_rows, :] for half in range(2)]
        for k in far:
            r_copy(ab, k).wait_recv()
            got = rr[ab, k].astype(F32)
            tot = [tot[half] + got[half * 8 : half * 8 + 8] for half in range(2)]
        for half in range(2):
            lo = ab * 1536 + half * 768
            fin = (tot[half] * gain_ref[:, lo : lo + 768] - rest8[:, lo : lo + 768]) / cnt8
            la_own[0, :, lo : lo + 768] = fin[0:4].astype(BF16)
            la_own[1, :, lo : lo + 768] = fin[4:8].astype(BF16)

    ld_la = pltpu.make_async_copy(la_own, outb_hbm.at[pl.ds(2 * z, 2)], load_sem.at[5])
    ld_la.start()
    la = {s: rcopy(la_own, outb_hbm.at[pl.ds(2 * z, 2)], l_send.at[s], l_recv.at[s], z_peer(s)) for s in z_order}
    for s in (4, 3, 5, 2, 6, 1, 7):
        la[s].start()
    for s in z_order:
        ea[s].wait_recv()
    ld_ea.wait()
    for s in z_order:
        la[s].wait_recv()
    for cp in live:
        cp.wait_send()
    ld_la.wait()


def body(images, gain, up_weight, down_weight, cotangent, seeds, assign):
    W = 3072 // NCH
    vm, dma = pltpu.VMEM, pltpu.SemaphoreType.DMA
    anyspace = pl.BlockSpec(memory_space=pl.ANY)
    early, late = pl.pallas_call(
        kernel,
        out_shape=[jax.ShapeDtypeStruct((16, 4, 3072), F32), jax.ShapeDtypeStruct((16, 4, 3072), BF16)],
        in_specs=[
            anyspace,
            pl.BlockSpec(memory_space=pltpu.VMEM),
            anyspace,
            anyspace,
            anyspace,
            pl.BlockSpec(memory_space=pltpu.SMEM),
            pl.BlockSpec(memory_space=pltpu.SMEM),
        ],
        out_specs=[anyspace, anyspace],
        scratch_shapes=[
            vm((3072, 768), BF16),
            vm((768, 3072), BF16),
            vm((2, 4, 3072), BF16),
            vm((16, 1536), F32),
            vm((2, 2, 4, 4, 16, 384), BF16),
            vm((8, 2, 2, 3072), BF16),
            vm((8, 8, 128), I32),
            vm((32, 3072), F32),
            vm((NCH, 2, 4, 4, 16, W), BF16),
            vm((2, 2, 512, 256), BF16),
            vm((16, 3072), I32),
            vm((512, 3072), F32),
            vm((528, 3072), BF16),
            vm((2, 256, 768), F32),
            vm((256, 768), F32),
            vm((16, 768), F32),
            vm((16, 768), F32),
            vm((256, 768), F32),
            vm((2, 256, 768), F32),
            vm((256, 768), F32),
            vm((2, 16, 128), F32),
            vm((2, 16, 128), F32),
            vm((2, 16, 128), F32),
            vm((2, 16, 128), F32),
            vm((2, 16, 128), F32),
            vm((256, 128), F32),
            vm((384, 256), BF16),
            vm((256, 768), BF16),
            vm((256, 768), BF16),
            vm((256, 768), BF16),
            vm((2, 2, 128, 768), F32),
            vm((2, 16, 16, 768), BF16),
            vm((2, 16, 16, 768), BF16),
            vm((2, 16, 128), F32),
            vm((3, 2, 16, 128), F32),
            vm((2, 16, 128), F32),
            vm((3, 2, 16, 128), F32),
            vm((16, 128), BF16),
            vm((2, 4, 3072), F32),
            vm((2, 4, 3072), BF16),
            dma((6,)),
            dma((8,)), dma((8,)),
            dma((8,)), dma((8,)),
            dma((2, 12)), dma((2, 12)),
            dma((NCH, 12)), dma((NCH, 12)),
            dma((6,)), dma((6,)),
            dma((2, 16)), dma((2, 16)),
            dma((6,)), dma((6,)),
            dma((8,)), dma((8,)),
            dma((8,)), dma((8,)),
        ],
        compiler_params=pltpu.CompilerParams(
            collective_id=0, has_side_effects=True, vmem_limit_bytes=56 * 1024 * 1024
        ),
        cost_estimate=pl.CostEstimate(flops=8 * 10**9, bytes_accessed=12 * 10**6, transcendentals=200000),
    )(images, gain.reshape(1, -1), up_weight, down_weight, cotangent, seeds, assign.reshape(-1))
    return early + late.astype(F32)


def solution(mesh):
    placed = (
        P("row", None, "col"),
        P("col"),
        P("col", "row"),
        P("row", "col"),
        P("row", "noise", "col"),
        P("noise"),
        P(),
    )
    return jax.shard_map(
        body, mesh=mesh, in_specs=placed, out_specs=P("row", None, "col"), check_vma=False
    )
```

time: 102 us -> 75.1 us (0.74)
  the two profiles are of different devices: /device:TPU:32 before, /device:TPU:1 now
where the time goes in v3:
time: 75.1 us; the launch traced here: 75 us
  Pallas kernels  72.8 us (97%)
  other arithmetic  2.18 us (3%)
    pallas_call x1, Pallas kernels, body(): pl.pallas_call(kernel, out_shape=[jax.ShapeDtypeStruct((16, 4, 3072), F32...  72.8 us
    add x1, other arithmetic, body(): return early + late.astype(F32)  2.18 us

profile of v3, /device:TPU:1, one launch (start us, length us, event | category | flops | bytes accessed | tf_op | source)
XLA Modules:
  0.0 75.0 jit_solution(17247690115543859239)
XLA Ops:
  0.0 72.8 %shard_map.73 = (f32[16,4,3072]{2,1,0:T(4,128)}, bf16[16,4,3072]{2,1,0:T(4,128)(2,1)}) custom-call(bf16[16,4,3072]{2,1,0:T(4,128)(2,1)} %img_hbm.1, f32[1,3072]{1,0:T(1,128)} %bitcast.7, bf16[3072,768]{1,0:T(8,128)(2,1)} %up_hbm.1, bf16[768,3072]{1,0:T(8,128)(2,1)} %dn_hbm.1, bf16[16,2,3072]{2,1,0:T(2,128)(2,1)} %cot_hbm.1, s32[2]{0:T(128)} %seeds_ref.1, ...), custom_call_target="tpu_custom_call" | custom-call | flops 8000000000 | bytes 12000000 | tf_op jit(solution)/shard_map/pallas_call | solution.py:511
  72.8 2.2 %convert_add_fusion = f32[8,8,3072]{2,1,0:T(8,128)} fusion(f32[8,8,3072]{2,1,0:T(8,128)} %bitcast.5, bf16[8,8,3072]{2,1,0:T(8,128)(2,1)} %bitcast.6), kind=kLoop, calls=%fused_computation | loop fusion | flops 393216 | bytes 1966080 | tf_op jit(solution)/shard_map/add | solution.py:581

commit v4 on v3

--- a/solution.py
+++ b/solution.py
@@ -1,4 +1,3 @@
-import functools
 import math
 
 import jax
@@ -9,7 +8,9 @@
 from jax.sharding import PartitionSpec as P
 
 D = 6144
-NCH = 4
+NJ = 2
+NCH = 2 * NJ
+WH = 3072 // (2 * NJ)
 noise_scale = 0.6
 gelu_coef = 0.044715
 root_term = math.sqrt(2.0 / math.pi)
@@ -62,12 +63,11 @@
 def kernel(
     img_hbm, gain_ref, up_hbm, dn_hbm, cot_hbm, seeds_ref, assign_ref, outa_hbm, outb_hbm,
     up_v, dn_v, img_own, pk16, imgg, rc, seedg, pk32, cg, onehot, base, noisy, scl,
-    pre, pre_in, ugp, ug_in, slope, bk, bk_in, stat, stat_in, mi, gst, gst_in, wt, wm, wx, wx_in, wall,
-    o_s, rs, rr, gx, gx_in, gy, gy_in, oh8, ea_own, la_own,
+    pre, pre_in, ugp, ug_in, slope, bk, bk_in, stat, stat_in, mi, gst, gst_in, wt, wm, hgb, wall,
+    o_s, rs, rr, gx, gx_in, gy, gy_in, ohs, ea_own, la_own,
     load_sem, z_send, z_recv, s_send, s_recv, i_send, i_recv, c_send, c_recv, k_send, k_recv,
     r_send, r_recv, g_send, g_recv, e_send, e_recv, l_send, l_recv,
 ):
-    W = 3072 // NCH
     z = lax.axis_index("noise")
     r = lax.axis_index("row")
     c = lax.axis_index("col")
@@ -171,18 +171,14 @@
     for s in range(16):
         for i in range(4):
             cnt[i] = cnt[i] + jnp.where(assign_ref[s] == i, 1.0, 0.0)
-    sub8 = lax.broadcasted_iota(I32, (8, 128), 0)
-    counts = jnp.zeros((8, 128), F32)
+    counts = jnp.ones((16, 128), F32)
     for i in range(4):
-        counts = jnp.where(lax.rem(sub8, 4) == i, cnt[i], counts)
-    cnt8 = counts[:, 0:1]
-    sel = jnp.zeros((8, 128), F32)
-    lane8 = lax.broadcasted_iota(I32, (8, 128), 1)
-    for tok in range(2):
-        for s in range(16):
-            hit = (lane8 == tok * 16 + s) & (sub8 == tok * 4 + assign_ref[s])
-            sel = jnp.where(hit, 1.0, sel)
-    oh8[...] = jnp.concatenate([sel, jnp.zeros((8, 128), F32)], axis=0).astype(BF16)
+        counts = jnp.where(sub16 == i, cnt[i], counts)
+    cnt4 = counts[0:4, 0:1]
+    sel = jnp.zeros((16, 128), F32)
+    for s in range(16):
+        sel = jnp.where((lane == s) & (sub16 == assign_ref[s]), 1.0, sel)
+    ohs[...] = sel.astype(BF16)
 
     def swap(b):
         return lax.rem(b, 4) * 4 + b // 4
@@ -194,7 +190,7 @@
             for half in range(2):
 
                 def fill(b, _, tok=tok, ab=ab, half=half):
-                    blk = b if tok == ab else swap(b)
+                    blk = b if ab == 0 else swap(b)
                     target = a16w + (blk * 16 + half * 8 + tok * 4)
                     onehot[ab, half, pl.ds(pl.multiple_of(tok * 256 + b * 16, 16), 16), :] = jnp.where(
                         col16 == target, 1.0, 0.0
@@ -216,10 +212,12 @@
             pk32[tok * 16 + 2 * k : tok * 16 + 2 * k + 2, :] = rc[k, tok].astype(F32)
     for j in range(NCH):
         for ab in range(2):
-            cg[j, ab, p2[ab], p1[ab]] = pk32[ab * 16 : (ab + 1) * 16, j * W : (j + 1) * W].astype(BF16)
+            tok, lo = j // NJ, (j % NJ) * 2 * WH + ab * WH
+            cg[j, ab, p2[ab], p1[ab]] = pk32[tok * 16 : tok * 16 + 16, lo : lo + WH].astype(BF16)
         cot_g[j].start(1)
-    early8 = dot_nn(oh8[:, 0:32], pk32[...].astype(BF16))[0:8] / cnt8
-    ea_own[0], ea_own[1] = early8[0:4], early8[4:8]
+    for tok in range(2):
+        early = dot_nn(ohs[:, 0:16], pk32[tok * 16 : tok * 16 + 16, :].astype(BF16))
+        ea_own[tok] = early[0:4] / cnt4
     ld_ea = pltpu.make_async_copy(ea_own, outa_hbm.at[pl.ds(2 * z, 2)], load_sem.at[4])
     ld_ea.start()
     ea = {s: rcopy(ea_own, outa_hbm.at[pl.ds(2 * z, 2)], e_send.at[s], e_recv.at[s], z_peer(s)) for s in z_order}
@@ -258,8 +256,7 @@
     pump(0)
 
     def token_of(tok, b):
-        rr = b if tok == 0 else swap(b)
-        return rr * 16 + z * 2 + tok
+        return b * 16 + z * 2 + tok
 
     def noise_block(tok, b, carry):
         tot, m2 = carry
@@ -294,7 +291,7 @@
     pump(3)
     carry = noise_blocks(1, 8, carry)
     stat[0], stat[1] = carry
-    cp_stat = rcopy(stat, stat_in, k_send.at[0], k_recv.at[0], other)
+    cp_stat = rcopy(stat, stat_in, k_send.at[1, 1], k_recv.at[1, 1], other)
     cp_stat.start()
     cp_stat.wait_recv()
     mean_a, mean_b = stat[0] * (1.0 / 3072.0), stat_in[0] * (1.0 / 3072.0)
@@ -320,192 +317,205 @@
 
     def pre_cols(n):
         res = dot_nn(scl[...], up_v[:, n * 256 : (n + 1) * 256])
-        pre[0, :, n * 256 : (n + 1) * 256] = res[0:256]
-        pre[1, :, n * 256 : (n + 1) * 256] = res[256:512]
+        for tok in range(2):
+            for h in range(2):
+                lo = tok * 256 + h * 128
+                pre[tok, h, :, n * 256 : (n + 1) * 256] = res[lo : lo + 128]
         ugp[:, n * 256 : (n + 1) * 256] = res[512:528]
 
     pre_cols(0)
     pre_cols(1)
     pre_cols(2)
-    cp_pre = rcopy(pre.at[1 - c], pre_in, k_send.at[1], k_recv.at[1], other)
-    cp_pre.start()
-    cp_ug = rcopy(ugp, ug_in, k_send.at[2], k_recv.at[2], other)
+    cp_pre = [
+        rcopy(pre.at[tok, 1 - c], pre_in.at[tok], k_send.at[0, tok], k_recv.at[0, tok], other) for tok in range(2)
+    ]
+    for cp in cp_pre:
+        cp.start()
+    cp_ug = rcopy(ugp, ug_in, k_send.at[1, 0], k_recv.at[1, 0], other)
     cp_ug.start()
 
-    def back_chunk(j, ab):
-        dim = cg[j, ab].reshape(256, W)
-        res = dot_nt(dim, dn_v[:, j * W : (j + 1) * W])
-        if j == 0:
-            bk[ab] = res
-        else:
-            bk[ab] = bk[ab] + res
-
-    for j in range(NCH - 1):
-        cot_g[j].wait(2)
+    def back_chunk(k):
+        tok = k // NJ
+        cot_g[k].wait(2)
         for ab in range(2):
-            back_chunk(j, ab)
-        if j == 0:
-            cp_pre.wait_recv()
-            cp_ug.wait_recv()
-        if j == 1:
-
-            def slope_block(k, _):
-                rows = pl.ds(pl.multiple_of(k * 16, 16), 16)
-                p = pre[c, rows, :] + pre_in[rows, :]
-                pre_in[rows, :] = p
-                slope[rows, :] = gelu_slope(p)
-                return 0
-
-            lax.fori_loop(0, 16, slope_block, 0)
-        if j == 2:
-            def wt_block(b, _):
-                rr = jnp.where(c == 0, b, swap(b))
-                inv = pick(mi[1], c * 16 + b)
-                wt[pl.ds(pl.multiple_of(b * 16, 16), 16), :] = jnp.where(
-                    lane == rr * 8 + c * 4 + a16, inv, 0.0
-                )
-                return 0
-
-            lax.fori_loop(0, 16, wt_block, 0)
-            full = wt[...].T
-            hi = full.astype(BF16)
-            mid = (full - hi.astype(F32)).astype(BF16)
-            lo = (full - hi.astype(F32) - mid.astype(F32)).astype(BF16)
-            wm[0:128] = hi
-            wm[128:256] = mid
-            wm[256:384] = lo
-    cot_g[NCH - 1].wait(2)
-    last = NCH - 1
-    for flip in (1, 0):
-        ab = (c + flip) % 2
-        dim = cg[last, ab].reshape(256, W)
-        bk[ab] = bk[ab] + dot_nt(dim, dn_v[:, last * W :])
-        if flip == 1:
-            cp_bk = rcopy(bk.at[1 - c], bk_in, k_send.at[3], k_recv.at[3], other)
-            cp_bk.start()
-    ug = (ugp[0:1] + ugp[1:2] + ugp[2:3]) + (ug_in[0:1] + ug_in[1:2] + ug_in[2:3])
-    cp_bk.wait_recv()
-
-    def hidden_block(b, carry):
-        gs, gd = carry
-        rows = pl.ds(pl.multiple_of(b * 16, 16), 16)
-        hg = ((bk[c, rows, :] + bk_in[rows, :]) * slope[rows, :]).astype(BF16)
-        scl[rows, 0:768] = hg
-        hf = hg.astype(F32)
-        s1 = jnp.sum(hf * ug, axis=1, keepdims=True)
-        s2 = jnp.sum(hf * pre_in[rows, :], axis=1, keepdims=True)
-        hit = lane == c * 16 + b
-        return jnp.where(hit, s1, gs), jnp.where(hit, s2, gd)
-
-    def hidden_blocks(k, carry):
-        for u in range(4):
-            carry = hidden_block(k * 4 + u, carry)
-        return carry
-
-    zero = jnp.zeros((16, 128), F32)
-    gst[0], gst[1] = lax.fori_loop(0, 4, hidden_blocks, (zero, zero))
-    cp_gst = rcopy(gst, gst_in, k_send.at[4], k_recv.at[4], other)
-    cp_gst.start()
-    wsum = dot_nn(wm[...], scl[0:256, 0:768])
-    wsum = wsum[0:128] + wsum[128:256] + wsum[256:384]
-    w_hi = wsum.astype(BF16)
-    wx[0:128] = w_hi
-    wx[128:256] = (wsum - w_hi.astype(F32)).astype(BF16)
-    cp_wx = rcopy(wx, wx_in, k_send.at[5], k_recv.at[5], other)
-    cp_wx.start()
-
-    cp_gst.wait_recv()
-    gx[...] = gst[...] + gst_in[...]
-
-    @functools.cache
-    def g_copy(axis, step):
+            lo = (k % NJ) * 2 * WH + ab * WH
+            res = dot_nt(cg[k, ab].reshape(256, WH), dn_v[:, lo : lo + WH])
+            for b in range(16):
+                at = b if ab == 0 else (b % 4) * 4 + b // 4
+                part = res[at * 16 : at * 16 + 16]
+                h, lb = b // 8, (b % 8) * 16
+                if k % NJ == 0 and ab == 0:
+                    bk[tok, h, lb : lb + 16] = part
+                else:
+                    bk[tok, h, lb : lb + 16] = bk[tok, h, lb : lb + 16] + part
+
+    cp_bk = [rcopy(bk.at[tok, 1 - c], bk_in.at[tok], k_send.at[2, tok], k_recv.at[2, tok], other) for tok in range(2)]
+    cp_gst = [rcopy(gst.at[tok], gst_in.at[tok], k_send.at[3, tok], k_recv.at[3, tok], other) for tok in range(2)]
+    cp_w = [
+        rcopy(wall.at[tok, c], wall.at[tok, c], k_send.at[4, tok], k_recv.at[4, tok], other) for tok in range(2)
+    ]
+
+    def g_copy(tok, axis, step):
         src, dst = ((gx, gx_in), (gy, gy_in))[axis]
         k = axis * 3 + step - 1
-        return rcopy(src, dst.at[step - 1], g_send.at[k], g_recv.at[k], row_peer(0, axis + 1, step))
-
-    for step in (1, 2, 3):
-        g_copy(0, step).start()
-
-    cp_wx.wait_recv()
-    wall[...] = (wx[...].astype(F32) + wx_in[...].astype(F32)).astype(BF16)
-
+        return rcopy(
+            src.at[tok], dst.at[tok, step - 1], g_send.at[tok, k], g_recv.at[tok, k], row_peer(0, axis + 1, step)
+        )
+
+    g_all = {
+        (tok, axis, step): g_copy(tok, axis, step) for tok in range(2) for axis in range(2) for step in (1, 2, 3)
+    }
     far = sorted(range(1, 16), key=lambda k: min(k // 4, 4 - k // 4) + min(k % 4, 4 - k % 4))
 
-    @functools.cache
-    def r_copy(ab, k):
+    def r_copy(tok, k):
         peer = wrap(y + k // 4, 4) * 4 + wrap(x + k % 4, 4)
-        return rcopy(rs.at[ab, peer], rr.at[ab, k], r_send.at[ab, k], r_recv.at[ab, k], {"row": peer})
-
-    for ab in range(2):
-        for half in range(2):
-            q = ab * 2 + half
-            o = dot_nt(wall[...], up_v[q * 768 : (q + 1) * 768, :])
-            o_s[ab, half] = o[0:128] + o[128:256]
-
-        def pack(k, _, ab=ab):
+        return rcopy(rs.at[tok, peer], rr.at[tok, k], r_send.at[tok, k], r_recv.at[tok, k], {"row": peer})
+
+    r_all = {(tok, k): r_copy(tok, k) for tok in range(2) for k in far}
+    la = {
+        (tok, s): rcopy(
+            la_own.at[tok], outb_hbm.at[2 * z + tok], l_send.at[tok, s], l_recv.at[tok, s], z_peer(s)
+        )
+        for tok in range(2)
+        for s in z_order
+    }
+
+    for tok in range(2):
+        cp_pre[tok].wait_recv()
+    cp_ug.wait_recv()
+    for tok in range(2):
+
+        def slope_block(k, _, tok=tok):
+            for u in range(2):
+                rows = pl.ds(pl.multiple_of(k * 32 + u * 16, 16), 16)
+                p = pre[tok, c, rows, :] + pre_in[tok, rows, :]
+                pre_in[tok, rows, :] = p
+                slope[tok, rows, :] = gelu_slope(p)
+            return 0
+
+        lax.fori_loop(0, 4, slope_block, 0)
+    ug = (ugp[0:1] + ugp[1:2] + ugp[2:3]) + (ug_in[0:1] + ug_in[1:2] + ug_in[2:3])
+    for tok in range(2):
+        for b in range(8):
+            inv = pick(mi[1], tok * 16 + c * 8 + b)
+            wt[b * 16 : b * 16 + 16, :] = jnp.where(lane == b * 4 + a16, inv, 0.0)
+        full = wt[...].T[0:32]
+        hi = full.astype(BF16)
+        mid = (full - hi.astype(F32)).astype(BF16)
+        lo = (full - hi.astype(F32) - mid.astype(F32)).astype(BF16)
+        wm[tok, 0:32] = hi
+        wm[tok, 32:64] = mid
+        wm[tok, 64:96] = lo
+
+    def hidden(tok):
+        cp_bk[tok].wait_recv()
+
+        def hidden_blocks(k, carry):
+            gs, gd = carry
+            for u in range(4):
+                b = k * 4 + u
+                rows = pl.ds(pl.multiple_of(b * 16, 16), 16)
+                hg = ((bk[tok, c, rows, :] + bk_in[tok, rows, :]) * slope[tok, rows, :]).astype(BF16)
+                hgb[tok, rows, :] = hg
+                hf = hg.astype(F32)
+                s1 = jnp.sum(hf * ug, axis=1, keepdims=True)
+                s2 = jnp.sum(hf * pre_in[tok, rows, :], axis=1, keepdims=True)
+                hit = lane == c * 8 + b
+                gs, gd = jnp.where(hit, s1, gs), jnp.where(hit, s2, gd)
+            return gs, gd
+
+        zero = jnp.zeros((16, 128), F32)
+        gst[tok, 0], gst[tok, 1] = lax.fori_loop(0, 2, hidden_blocks, (zero, zero))
+        wsum = dot_nn(wm[tok], hgb[tok])
+        wsum = wsum[0:32] + wsum[32:64] + wsum[64:96]
+        w_hi = wsum.astype(BF16)
+        wall[tok, c, 0] = w_hi
+        wall[tok, c, 1] = (wsum - w_hi.astype(F32)).astype(BF16)
+        cp_w[tok].start()
+        cp_gst[tok].start()
+
+    def spread(tok):
+        cp_w[tok].wait_recv()
+        cp_gst[tok].wait_recv()
+        gx[tok] = gst[tok] + gst_in[tok]
+        for step in (1, 2, 3):
+            g_all[tok, 0, step].start()
+        for q in range(4):
+            o = dot_nt(wall[tok].reshape(128, 768), up_v[q * 768 : (q + 1) * 768, :])
+            o_s[tok, q, 0:32] = o[0:32] + o[32:64]
+            o_s[tok, q, 32:64] = o[64:96] + o[96:128]
+
+        def pack(k, _):
             rows = pl.ds(pl.multiple_of(k * 8, 8), 8)
-            both = jnp.concatenate([o_s[ab, 0, rows, :], o_s[ab, 1, rows, :]], axis=0)
-            rs[ab, k] = both.astype(BF16)
+            v = [o_s[tok, q, rows, :] for q in range(4)]
+            for u in range(2):
+                rs[tok, k * 2 + u] = jnp.concatenate([w[u * 4 : u * 4 + 4] for w in v], axis=0).astype(BF16)
             return 0
 
-        lax.fori_loop(0, 16, pack, 0)
+        lax.fori_loop(0, 8, pack, 0)
         for k in far:
-            r_copy(ab, k).start()
-        if ab == 0:
-            for step in (1, 2, 3):
-                g_copy(0, step).wait_recv()
-            gy[...] = gx[...] + gx_in[0] + gx_in[1] + gx_in[2]
-            for step in (1, 2, 3):
-                g_copy(1, step).start()
-
-    for step in (1, 2, 3):
-        g_copy(1, step).wait_recv()
-    gtot = (gy[...] + gy_in[0] + gy_in[1] + gy_in[2]) * (1.0 / D)
-    own_b = (y * 4 + x, x * 4 + y)
-    for tok in range(2):
-        k = tok * 16 + own_b[tok]
-        rows = pl.ds(pl.multiple_of(tok * 256 + own_b[tok] * 16, 16), 16)
-        inv = pick(mi[1], k)
-        normed = (noisy[rows, :] - pick(mi[0], k)) * inv
-        v = inv * (pick(gtot[0], k) + normed * pick(gtot[1], k))
-        pk32[tok * 16 : tok * 16 + 16, :] = v
-    rest = pk32[...]
-    t1 = rest.astype(BF16)
-    t2 = (rest - t1.astype(F32)).astype(BF16)
-    t3 = (rest - t1.astype(F32) - t2.astype(F32)).astype(BF16)
-    pick8 = oh8[:, 0:32]
-    rest8 = (dot_nn(pick8, t1) + dot_nn(pick8, t2) + dot_nn(pick8, t3))[0:8]
-
-    own_rows = pl.ds(pl.multiple_of(r * 8, 8), 8)
-    for ab in range(2):
-        tot = [o_s[ab, half, own_rows, :] for half in range(2)]
+            r_all[tok, k].start()
+
+    def sums_y(tok):
+        for step in (1, 2, 3):
+            g_all[tok, 0, step].wait_recv()
+        gy[tok] = gx[tok] + gx_in[tok, 0] + gx_in[tok, 1] + gx_in[tok, 2]
+        for step in (1, 2, 3):
+            g_all[tok, 1, step].start()
+
+    def finish(tok):
+        for step in (1, 2, 3):
+            g_all[tok, 1, step].wait_recv()
+        gtot = (gy[tok] + gy_in[tok, 0] + gy_in[tok, 1] + gy_in[tok, 2]) * (1.0 / D)
+        rows = pl.ds(pl.multiple_of(tok * 256 + r * 16, 16), 16)
+        inv = pick(mi[1], tok * 16 + r)
+        normed = (noisy[rows, :] - pick(mi[0], tok * 16 + r)) * inv
+        v = inv * (pick(gtot[0], r) + normed * pick(gtot[1], r))
+        t1 = v.astype(BF16)
+        t2 = (v - t1.astype(F32)).astype(BF16)
+        t3 = (v - t1.astype(F32) - t2.astype(F32)).astype(BF16)
+        one = ohs[:, 0:16]
+        rest4 = (dot_nn(one, t1) + dot_nn(one, t2) + dot_nn(one, t3))[0:4]
+        tot = rs[tok, r].astype(F32)
         for k in far:
-            r_copy(ab, k).wait_recv()
-            got = rr[ab, k].astype(F32)
-            tot = [tot[half] + got[half * 8 : half * 8 + 8] for half in range(2)]
-        for half in range(2):
-            lo = ab * 1536 + half * 768
-            fin = (tot[half] * gain_ref[:, lo : lo + 768] - rest8[:, lo : lo + 768]) / cnt8
-            la_own[0, :, lo : lo + 768] = fin[0:4].astype(BF16)
-            la_own[1, :, lo : lo + 768] = fin[4:8].astype(BF16)
-
+            r_all[tok, k].wait_recv()
+            tot = tot + rr[tok, k].astype(F32)
+        for q in range(4):
+            lo = q * 768
+            fin = (tot[q * 4 : q * 4 + 4] * gain_ref[:, lo : lo + 768] - rest4[:, lo : lo + 768]) / cnt4
+            la_own[tok, :, lo : lo + 768] = fin.astype(BF16)
+        for s in (4, 3, 5, 2, 6, 1, 7):
+            la[tok, s].start()
+
+    for k in range(NJ):
+        back_chunk(k)
+    cp_bk[0].start()
+    hidden(0)
+    spread(0)
+    back_chunk(NJ)
+    sums_y(0)
+    for k in range(NJ + 1, NCH):
+        back_chunk(k)
+    cp_bk[1].start()
+    hidden(1)
+    finish(0)
+    spread(1)
+    sums_y(1)
+    finish(1)
     ld_la = pltpu.make_async_copy(la_own, outb_hbm.at[pl.ds(2 * z, 2)], load_sem.at[5])
     ld_la.start()
-    la = {s: rcopy(la_own, outb_hbm.at[pl.ds(2 * z, 2)], l_send.at[s], l_recv.at[s], z_peer(s)) for s in z_order}
-    for s in (4, 3, 5, 2, 6, 1, 7):
-        la[s].start()
     for s in z_order:
         ea[s].wait_recv()
     ld_ea.wait()
-    for s in z_order:
-        la[s].wait_recv()
+    for tok in range(2):
+        for s in z_order:
+            la[tok, s].wait_recv()
     for cp in live:
         cp.wait_send()
     ld_la.wait()
 
 
 def body(images, gain, up_weight, down_weight, cotangent, seeds, assign):
-    W = 3072 // NCH
     vm, dma = pltpu.VMEM, pltpu.SemaphoreType.DMA
     anyspace = pl.BlockSpec(memory_space=pl.ANY)
     early, late = pl.pallas_call(
@@ -530,35 +540,34 @@
             vm((8, 2, 2, 3072), BF16),
             vm((8, 8, 128), I32),
             vm((32, 3072), F32),
-            vm((NCH, 2, 4, 4, 16, W), BF16),
+            vm((NCH, 2, 4, 4, 16, WH), BF16),
             vm((2, 2, 512, 256), BF16),
             vm((16, 3072), I32),
             vm((512, 3072), F32),
             vm((528, 3072), BF16),
-            vm((2, 256, 768), F32),
-            vm((256, 768), F32),
+            vm((2, 2, 128, 768), F32),
+            vm((2, 128, 768), F32),
             vm((16, 768), F32),
             vm((16, 768), F32),
-            vm((256, 768), F32),
-            vm((2, 256, 768), F32),
-            vm((256, 768), F32),
+            vm((2, 128, 768), F32),
+            vm((2, 2, 128, 768), F32),
+            vm((2, 128, 768), F32),
             vm((2, 16, 128), F32),
             vm((2, 16, 128), F32),
             vm((2, 16, 128), F32),
-            vm((2, 16, 128), F32),
-            vm((2, 16, 128), F32),
-            vm((256, 128), F32),
-            vm((384, 256), BF16),
-            vm((256, 768), BF16),
-            vm((256, 768), BF16),
-            vm((256, 768), BF16),
-            vm((2, 2, 128, 768), F32),
+            vm((2, 2, 16, 128), F32),
+            vm((2, 2, 16, 128), F32),
+            vm((128, 128), F32),
+            vm((2, 96, 128), BF16),
+            vm((2, 128, 768), BF16),
+            vm((2, 2, 2, 32, 768), BF16),
+            vm((2, 4, 64, 768), F32),
             vm((2, 16, 16, 768), BF16),
             vm((2, 16, 16, 768), BF16),
-            vm((2, 16, 128), F32),
-            vm((3, 2, 16, 128), F32),
-            vm((2, 16, 128), F32),
-            vm((3, 2, 16, 128), F32),
+            vm((2, 2, 16, 128), F32),
+            vm((2, 3, 2, 16, 128), F32),
+            vm((2, 2, 16, 128), F32),
+            vm((2, 3, 2, 16, 128), F32),
             vm((16, 128), BF16),
             vm((2, 4, 3072), F32),
             vm((2, 4, 3072), BF16),
@@ -567,11 +576,11 @@
             dma((8,)), dma((8,)),
             dma((2, 12)), dma((2, 12)),
             dma((NCH, 12)), dma((NCH, 12)),
-            dma((6,)), dma((6,)),
+            dma((5, 2)), dma((5, 2)),
             dma((2, 16)), dma((2, 16)),
-            dma((6,)), dma((6,)),
+            dma((2, 6)), dma((2, 6)),
             dma((8,)), dma((8,)),
-            dma((8,)), dma((8,)),
+            dma((2, 8)), dma((2, 8)),
         ],
         compiler_params=pltpu.CompilerParams(
             collective_id=0, has_side_effects=True, vmem_limit_bytes=56 * 1024 * 1024

time: 75.1 us -> 70.4 us (0.937)
  the two profiles are of different devices: /device:TPU:1 before, /device:TPU:32 now
where the time goes in v4:
time: 70.4 us; the launch traced here: 70.3 us
  Pallas kernels  68.1 us (97%)
  other arithmetic  2.18 us (3%)
    pallas_call x1, Pallas kernels, body(): pl.pallas_call(kernel, out_shape=[jax.ShapeDtypeStruct((16, 4, 3072), F32...  68.1 us
    add x1, other arithmetic, body(): return early + late.astype(F32)  2.18 us

profile of v4, /device:TPU:32, one launch (start us, length us, event | category | flops | bytes accessed | tf_op | source)
XLA Modules:
  0.0 70.3 jit_solution(6901836319434072220)
XLA Ops:
  0.0 68.1 %shard_map.73 = (f32[16,4,3072]{2,1,0:T(4,128)}, bf16[16,4,3072]{2,1,0:T(4,128)(2,1)}) custom-call(bf16[16,4,3072]{2,1,0:T(4,128)(2,1)} %img_hbm.1, f32[1,3072]{1,0:T(1,128)} %bitcast.7, bf16[3072,768]{1,0:T(8,128)(2,1)} %up_hbm.1, bf16[768,3072]{1,0:T(8,128)(2,1)} %dn_hbm.1, bf16[16,2,3072]{2,1,0:T(2,128)(2,1)} %cot_hbm.1, s32[2]{0:T(128)} %seeds_ref.1, ...), custom_call_target="tpu_custom_call" | custom-call | flops 8000000000 | bytes 12000000 | tf_op jit(solution)/shard_map/pallas_call | solution.py:521
  68.1 2.2 %convert_add_fusion = f32[8,8,3072]{2,1,0:T(8,128)} fusion(f32[8,8,3072]{2,1,0:T(8,128)} %bitcast.5, bf16[8,8,3072]{2,1,0:T(8,128)(2,1)} %bitcast.6), kind=kLoop, calls=%fused_computation | loop fusion | flops 393216 | bytes 1966080 | tf_op jit(solution)/shard_map/add | solution.py:590

commit v5 on v4

--- a/solution.py
+++ b/solution.py
@@ -8,9 +8,6 @@
 from jax.sharding import PartitionSpec as P
 
 D = 6144
-NJ = 2
-NCH = 2 * NJ
-WH = 3072 // (2 * NJ)
 noise_scale = 0.6
 gelu_coef = 0.044715
 root_term = math.sqrt(2.0 / math.pi)
@@ -36,24 +33,31 @@
     return lax.dot_general(a, b, (((1,), (0,)), ((), ())), preferred_element_type=F32)
 
 
-class Copy:
+class Copies:
+    def __init__(self, live, ssem, rsem, whole, dev):
+        self.live, self.ssem, self.rsem = live, ssem, rsem
+        self.whole = lambda: pltpu.make_async_remote_copy(
+            src_ref=whole, dst_ref=whole, send_sem=ssem, recv_sem=rsem, device_id=dev, device_id_type=MESH
+        )
+
+    def send(self, src, dst, dev):
+        if self not in self.live:
+            self.live.append(self)
+        pltpu.make_async_remote_copy(
+            src_ref=src, dst_ref=dst, send_sem=self.ssem, recv_sem=self.rsem, device_id=dev, device_id_type=MESH
+        ).start()
+
+    def wait_recv(self):
+        self.whole().wait_recv()
+
+    def wait_send(self):
+        self.whole().wait_send()
+
+
+class Copy(Copies):
     def __init__(self, live, src, dst, ssem, rsem, dev):
-        self.live, self.got = live, False
-        self.make = lambda: pltpu.make_async_remote_copy(
-            src_ref=src, dst_ref=dst, send_sem=ssem, recv_sem=rsem, device_id=dev, device_id_type=MESH
-        )
-
-    def start(self):
-        self.made = self.make()
-        self.made.start()
-        self.live.append(self)
-
-    def wait_recv(self):
-        self.made.wait_recv()
-        self.got = True
-
-    def wait_send(self):
-        self.made.wait_send()
+        super().__init__(live, ssem, rsem, dst, dev)
+        self.start = lambda: self.send(src, dst, dev)
 
 
 def wrap(i, n):
@@ -65,7 +69,7 @@
     up_v, dn_v, img_own, pk16, imgg, rc, seedg, pk32, cg, onehot, base, noisy, scl,
     pre, pre_in, ugp, ug_in, slope, bk, bk_in, stat, stat_in, mi, gst, gst_in, wt, wm, hgb, wall,
     o_s, rs, rr, gx, gx_in, gy, gy_in, ohs, ea_own, la_own,
-    load_sem, z_send, z_recv, s_send, s_recv, i_send, i_recv, c_send, c_recv, k_send, k_recv,
+    load_sem, z_send, z_recv, i_send, i_recv, c_send, c_recv, k_send, k_recv,
     r_send, r_recv, g_send, g_recv, e_send, e_recv, l_send, l_recv,
 ):
     z = lax.axis_index("noise")
@@ -119,48 +123,40 @@
             pk16[half * 8 + tok * 4 : half * 8 + tok * 4 + 4, ab * 768 : (ab + 1) * 768] = v[
                 :, q * 768 : (q + 1) * 768
             ]
-    for ch in range(2):
-        for ab in range(2):
-            lo = ab * 768 + ch * 384
-            imgg[ch, ab, p2[ab], p1[ab]] = pk16[:, lo : lo + 384].astype(BF16)
+    for ab in range(2):
+        imgg[ab, p2[ab], p1[ab]] = pk16[:, ab * 768 : ab * 768 + 768].astype(BF16)
     pl.semaphore_wait(barrier, 23)
 
     z_order = (1, 7, 2, 6, 3, 5, 4)
-    z_cot, z_seed = {}, {}
+    z_seed = Copies(live, z_send.at[0], z_recv.at[0], seedg.at[pl.ds(0, 7)], z_peer(1))
+    z_cot = Copies(live, z_send.at[1], z_recv.at[1], rc.at[pl.ds(0, 7)], z_peer(1))
     for s in z_order:
-        peer = wrap(z + s, 8)
-        z_cot[s] = rcopy(cot_hbm.at[pl.ds(2 * peer, 2)], rc.at[z], z_send.at[s], z_recv.at[s], z_peer(s))
-        z_seed[s] = rcopy(seedg.at[z], seedg.at[z], s_send.at[s], s_recv.at[s], z_peer(s))
-        z_cot[s].start()
-        z_seed[s].start()
+        z_seed.send(seedg.at[z], seedg.at[z], z_peer(s))
+    for s in z_order:
+        z_cot.send(cot_hbm.at[pl.ds(2 * wrap(z + s, 8), 2)], rc.at[z], z_peer(s))
 
     class Gather:
         def __init__(self, buf, ssem, rsem):
-            self.copies = {}
-            for ab in range(2):
-                for phase in (1, 2):
-                    own = buf.at[ab, p2[ab], p1[ab]] if phase == 1 else buf.at[ab, p2[ab]]
-                    for step in (1, 3, 2):
-                        k = (ab * 2 + phase - 1) * 3 + step - 1
-                        self.copies[ab, phase, step] = rcopy(
-                            own, own, ssem.at[k], rsem.at[k], row_peer(ab, phase, step)
-                        )
+            three = pl.ds(0, 3)
+            whole = (buf.at[pl.ds(0, 2), 0, three], buf.at[pl.ds(0, 2), three])
+            self.buf = buf
+            self.copies = [
+                Copies(live, ssem.at[n], rsem.at[n], whole[n], row_peer(0, n + 1, 1)) for n in range(2)
+            ]
 
         def start(self, phase):
             for step in (1, 3, 2):
                 for ab in range(2):
-                    self.copies[ab, phase, step].start()
+                    own = self.buf.at[ab, p2[ab], p1[ab]] if phase == 1 else self.buf.at[ab, p2[ab]]
+                    self.copies[phase - 1].send(own, own, row_peer(ab, phase, step))
 
         def wait(self, phase):
-            for step in (1, 3, 2):
-                for ab in range(2):
-                    self.copies[ab, phase, step].wait_recv()
-
-    img_g = [Gather(imgg.at[ch], i_send.at[ch], i_recv.at[ch]) for ch in range(2)]
-    cot_g = [Gather(cg.at[j], c_send.at[j], c_recv.at[j]) for j in range(NCH)]
-
-    for g in img_g:
-        g.start(1)
+            self.copies[phase - 1].wait_recv()
+
+    img_g = Gather(imgg, i_send, i_recv)
+    cot_g = [Gather(cg.at[j], c_send.at[j], c_recv.at[j]) for j in range(2)]
+
+    img_g.start(1)
 
     sub16 = lax.broadcasted_iota(I32, (16, 128), 0)
     lane = lax.broadcasted_iota(I32, (16, 128), 1)
@@ -199,37 +195,8 @@
 
                 lax.fori_loop(0, 16, fill, 0)
 
-    for g in img_g:
-        g.wait(1)
-        g.start(2)
-
-    for s in z_order:
-        z_cot[s].wait_recv()
-        z_seed[s].wait_recv()
-    ld_cot.wait()
-    for k in range(8):
-        for tok in range(2):
-            pk32[tok * 16 + 2 * k : tok * 16 + 2 * k + 2, :] = rc[k, tok].astype(F32)
-    for j in range(NCH):
-        for ab in range(2):
-            tok, lo = j // NJ, (j % NJ) * 2 * WH + ab * WH
-            cg[j, ab, p2[ab], p1[ab]] = pk32[tok * 16 : tok * 16 + 16, lo : lo + WH].astype(BF16)
-        cot_g[j].start(1)
-    for tok in range(2):
-        early = dot_nn(ohs[:, 0:16], pk32[tok * 16 : tok * 16 + 16, :].astype(BF16))
-        ea_own[tok] = early[0:4] / cnt4
-    ld_ea = pltpu.make_async_copy(ea_own, outa_hbm.at[pl.ds(2 * z, 2)], load_sem.at[4])
-    ld_ea.start()
-    ea = {s: rcopy(ea_own, outa_hbm.at[pl.ds(2 * z, 2)], e_send.at[s], e_recv.at[s], z_peer(s)) for s in z_order}
-    for s in z_order:
-        ea[s].start()
-
-    for k in range(8):
-        for e in range(2):
-            s = 2 * k + e
-            pos = lax.broadcasted_iota(I32, (1, 3072), 1)
-            row = seedg[k, e : e + 1, 0:1] * 1013904223
-            base[s : s + 1, :] = (pos + c * 3072) * 1664525 + row
+    img_g.wait(1)
+    img_g.start(2)
 
     g0 = gain_ref[...]
     g_hi = g0.astype(BF16)
@@ -241,55 +208,76 @@
         g_hi.astype(F32),
         jnp.where(sub_g == 1, g_mid.astype(F32), jnp.where(sub_g == 2, g_lo.astype(F32), 0.0)),
     ).astype(BF16)
-
-    for ch in range(2):
-        img_g[ch].wait(2)
+    z_seed.wait_recv()
+    for k in range(8):
+        for e in range(2):
+            s = 2 * k + e
+            pos = lax.broadcasted_iota(I32, (1, 3072), 1)
+            row = seedg[k, e : e + 1, 0:1] * 1013904223
+            base[s : s + 1, :] = (pos + c * 3072) * 1664525 + row
+
+    def field_blocks(tok):
+        def four(k, _):
+            for u in range(4):
+                b = k * 4 + u
+                mixed = base[...] + (b * 16 + z * 2 + tok) * D * 1664525
+                mixed = mixed ^ (mixed >> 13)
+                mixed = mixed * 1274126177
+                mixed = mixed ^ (mixed >> 16)
+                field = (mixed & 65535).astype(F32) - 32767.5
+                noisy[pl.ds(pl.multiple_of(tok * 256 + b * 16, 16), 16), :] = field * (noise_scale / 18918.0)
+            return 0
+
+        lax.fori_loop(0, 4, four, 0)
+
+    def pack_cot(tok):
+        for k in range(8):
+            pk32[tok * 16 + 2 * k : tok * 16 + 2 * k + 2, :] = rc[k, tok].astype(F32)
         for ab in range(2):
-            for half in range(2):
-                lo = ab * 1536 + half * 768 + ch * 384
-                noisy[:, lo : lo + 384] = dot_nn(onehot[ab, half], imgg[ch, ab].reshape(256, 384))
+            cg[tok, ab, p2[ab], p1[ab]] = pk32[tok * 16 : tok * 16 + 16, ab * 1536 : ab * 1536 + 1536].astype(BF16)
+        cot_g[tok].start(1)
 
     def pump(k):
         cot_g[k].wait(1)
         cot_g[k].start(2)
 
+    z_cot.wait_recv()
+    ld_cot.wait()
+    pack_cot(0)
+    pack_cot(1)
+    for tok in range(2):
+        early = dot_nn(ohs[:, 0:16], pk32[tok * 16 : tok * 16 + 16, :].astype(BF16))
+        ea_own[tok] = early[0:4] / cnt4
+    ld_ea = pltpu.make_async_copy(ea_own, outa_hbm.at[pl.ds(2 * z, 2)], load_sem.at[4])
+    ld_ea.start()
+    ea = Copies(live, e_send.at[0], e_recv.at[0], outa_hbm.at[pl.ds(0, 14)], z_peer(1))
+    for s in z_order:
+        ea.send(ea_own, outa_hbm.at[pl.ds(2 * z, 2)], z_peer(s))
+    field_blocks(0)
+    field_blocks(1)
     pump(0)
-
-    def token_of(tok, b):
-        return b * 16 + z * 2 + tok
-
-    def noise_block(tok, b, carry):
+    img_g.wait(2)
+    for ab in range(2):
+        for half in range(2):
+            lo = ab * 1536 + half * 768
+            noisy[:, lo : lo + 768] = noisy[:, lo : lo + 768] + dot_nn(
+                onehot[ab, half], imgg[ab].reshape(256, 768)
+            )
+    pump(1)
+
+    def stat_blocks(k, carry):
         tot, m2 = carry
-        rows = pl.ds(pl.multiple_of(tok * 256 + b * 16, 16), 16)
-        mixed = base[...] + token_of(tok, b) * D * 1664525
-        mixed = mixed ^ (mixed >> 13)
-        mixed = mixed * 1274126177
-        mixed = mixed ^ (mixed >> 16)
-        field = (mixed & 65535).astype(F32) - 32767.5
-        v = noisy[rows, :] + field * (noise_scale / 18918.0)
-        noisy[rows, :] = v
-        s1 = jnp.sum(v, axis=1, keepdims=True)
-        dev = v - s1 * (1.0 / 3072.0)
-        s2 = jnp.sum(dev * dev, axis=1, keepdims=True)
-        hit = lane == tok * 16 + b
-        return jnp.where(hit, s1, tot), jnp.where(hit, s2, m2)
-
-    carry = (jnp.zeros((16, 128), F32), jnp.zeros((16, 128), F32))
-    def noise_blocks(tok, first, carry):
-        def four(k, cr):
-            for u in range(4):
-                cr = noise_block(tok, first + k * 4 + u, cr)
-            return cr
-
-        return lax.fori_loop(0, 2, four, carry)
-
-    carry = noise_blocks(0, 0, carry)
-    pump(1)
-    carry = noise_blocks(0, 8, carry)
-    pump(2)
-    carry = noise_blocks(1, 0, carry)
-    pump(3)
-    carry = noise_blocks(1, 8, carry)
+        for u in range(4):
+            n = k * 4 + u
+            v = noisy[pl.ds(pl.multiple_of(n * 16, 16), 16), :]
+            s1 = jnp.sum(v, axis=1, keepdims=True)
+            dev = v - s1 * (1.0 / 3072.0)
+            s2 = jnp.sum(dev * dev, axis=1, keepdims=True)
+            hit = lane == n
+            tot, m2 = jnp.where(hit, s1, tot), jnp.where(hit, s2, m2)
+        return tot, m2
+
+    carry = lax.fori_loop(0, 8, stat_blocks, (jnp.zeros((16, 128), F32), jnp.zeros((16, 128), F32)))
     stat[0], stat[1] = carry
     cp_stat = rcopy(stat, stat_in, k_send.at[1, 1], k_recv.at[1, 1], other)
     cp_stat.start()
@@ -334,17 +322,16 @@
     cp_ug = rcopy(ugp, ug_in, k_send.at[1, 0], k_recv.at[1, 0], other)
     cp_ug.start()
 
-    def back_chunk(k):
-        tok = k // NJ
-        cot_g[k].wait(2)
+    def back_part(tok):
+        cot_g[tok].wait(2)
         for ab in range(2):
-            lo = (k % NJ) * 2 * WH + ab * WH
-            res = dot_nt(cg[k, ab].reshape(256, WH), dn_v[:, lo : lo + WH])
+            lo = ab * 1536
+            res = dot_nt(cg[tok, ab].reshape(256, 1536), dn_v[:, lo : lo + 1536])
             for b in range(16):
                 at = b if ab == 0 else (b % 4) * 4 + b // 4
                 part = res[at * 16 : at * 16 + 16]
                 h, lb = b // 8, (b % 8) * 16
-                if k % NJ == 0 and ab == 0:
+                if ab == 0:
                     bk[tok, h, lb : lb + 16] = part
                 else:
                     bk[tok, h, lb : lb + 16] = bk[tok, h, lb : lb + 16] + part
@@ -355,30 +342,26 @@
         rcopy(wall.at[tok, c], wall.at[tok, c], k_send.at[4, tok], k_recv.at[4, tok], other) for tok in range(2)
     ]
 
-    def g_copy(tok, axis, step):
-        src, dst = ((gx, gx_in), (gy, gy_in))[axis]
-        k = axis * 3 + step - 1
-        return rcopy(
-            src.at[tok], dst.at[tok, step - 1], g_send.at[tok, k], g_recv.at[tok, k], row_peer(0, axis + 1, step)
-        )
-
-    g_all = {
-        (tok, axis, step): g_copy(tok, axis, step) for tok in range(2) for axis in range(2) for step in (1, 2, 3)
-    }
-    far = sorted(range(1, 16), key=lambda k: min(k // 4, 4 - k // 4) + min(k % 4, 4 - k % 4))
-
-    def r_copy(tok, k):
-        peer = wrap(y + k // 4, 4) * 4 + wrap(x + k % 4, 4)
-        return rcopy(rs.at[tok, peer], rr.at[tok, k], r_send.at[tok, k], r_recv.at[tok, k], {"row": peer})
-
-    r_all = {(tok, k): r_copy(tok, k) for tok in range(2) for k in far}
-    la = {
-        (tok, s): rcopy(
-            la_own.at[tok], outb_hbm.at[2 * z + tok], l_send.at[tok, s], l_recv.at[tok, s], z_peer(s)
+    sums = {
+        (tok, axis): Copies(
+            live, g_send.at[tok, axis], g_recv.at[tok, axis], (gx_in, gy_in)[axis].at[tok], row_peer(0, axis + 1, 1)
         )
         for tok in range(2)
-        for s in z_order
+        for axis in range(2)
     }
+
+    def sums_send(tok, axis):
+        src, dst = ((gx, gx_in), (gy, gy_in))[axis]
+        for step in (1, 3, 2):
+            sums[tok, axis].send(src.at[tok], dst.at[tok, step - 1], row_peer(0, axis + 1, step))
+
+    far = sorted(range(1, 16), key=lambda k: min(k // 4, 4 - k // 4) + min(k % 4, 4 - k % 4))
+    parts = [
+        Copies(live, r_send.at[tok], r_recv.at[tok], rr.at[tok, pl.ds(1, 15)], row_peer(0, 1, 1)) for tok in range(2)
+    ]
+    late = [
+        Copies(live, l_send.at[tok], l_recv.at[tok], outb_hbm.at[pl.ds(0, 7)], z_peer(1)) for tok in range(2)
+    ]
 
     for tok in range(2):
         cp_pre[tok].wait_recv()
@@ -438,8 +421,7 @@
         cp_w[tok].wait_recv()
         cp_gst[tok].wait_recv()
         gx[tok] = gst[tok] + gst_in[tok]
-        for step in (1, 2, 3):
-            g_all[tok, 0, step].start()
+        sums_send(tok, 0)
         for q in range(4):
             o = dot_nt(wall[tok].reshape(128, 768), up_v[q * 768 : (q + 1) * 768, :])
             o_s[tok, q, 0:32] = o[0:32] + o[32:64]
@@ -454,18 +436,16 @@
 
         lax.fori_loop(0, 8, pack, 0)
         for k in far:
-            r_all[tok, k].start()
+            peer = wrap(y + k // 4, 4) * 4 + wrap(x + k % 4, 4)
+            parts[tok].send(rs.at[tok, peer], rr.at[tok, k], {"row": peer})
 
     def sums_y(tok):
-        for step in (1, 2, 3):
-            g_all[tok, 0, step].wait_recv()
+        sums[tok, 0].wait_recv()
         gy[tok] = gx[tok] + gx_in[tok, 0] + gx_in[tok, 1] + gx_in[tok, 2]
-        for step in (1, 2, 3):
-            g_all[tok, 1, step].start()
+        sums_send(tok, 1)
 
     def finish(tok):
-        for step in (1, 2, 3):
-            g_all[tok, 1, step].wait_recv()
+        sums[tok, 1].wait_recv()
         gtot = (gy[tok] + gy_in[tok, 0] + gy_in[tok, 1] + gy_in[tok, 2]) * (1.0 / D)
         rows = pl.ds(pl.multiple_of(tok * 256 + r * 16, 16), 16)
         inv = pick(mi[1], tok * 16 + r)
@@ -477,40 +457,39 @@
         one = ohs[:, 0:16]
         rest4 = (dot_nn(one, t1) + dot_nn(one, t2) + dot_nn(one, t3))[0:4]
         tot = rs[tok, r].astype(F32)
-        for k in far:
-            r_all[tok, k].wait_recv()
+        parts[tok].wait_recv()
+        for k in range(1, 16):
             tot = tot + rr[tok, k].astype(F32)
         for q in range(4):
             lo = q * 768
             fin = (tot[q * 4 : q * 4 + 4] * gain_ref[:, lo : lo + 768] - rest4[:, lo : lo + 768]) / cnt4
             la_own[tok, :, lo : lo + 768] = fin.astype(BF16)
         for s in (4, 3, 5, 2, 6, 1, 7):
-            la[tok, s].start()
-
-    for k in range(NJ):
-        back_chunk(k)
+            late[tok].send(la_own.at[tok], outb_hbm.at[2 * z + tok], z_peer(s))
+
+    back_part(0)
     cp_bk[0].start()
     hidden(0)
     spread(0)
-    back_chunk(NJ)
     sums_y(0)
-    for k in range(NJ + 1, NCH):
-        back_chunk(k)
+    back_part(1)
     cp_bk[1].start()
     hidden(1)
     finish(0)
     spread(1)
     sums_y(1)
+    ea.wait_recv()
+    ld_ea.wait()
+    old = [cp for cp in live if cp is not parts[1] and cp is not sums[1, 1]]
+    for cp in old:
+        if cp is not late[0]:
+            cp.wait_send()
     finish(1)
     ld_la = pltpu.make_async_copy(la_own, outb_hbm.at[pl.ds(2 * z, 2)], load_sem.at[5])
     ld_la.start()
-    for s in z_order:
-        ea[s].wait_recv()
-    ld_ea.wait()
-    for tok in range(2):
-        for s in z_order:
-            la[tok, s].wait_recv()
-    for cp in live:
+    for tok in range(2):
+        late[tok].wait_recv()
+    for cp in (parts[1], sums[1, 1], late[0], late[1]):
         cp.wait_send()
     ld_la.wait()
 
@@ -536,11 +515,11 @@
             vm((768, 3072), BF16),
             vm((2, 4, 3072), BF16),
             vm((16, 1536), F32),
-            vm((2, 2, 4, 4, 16, 384), BF16),
+            vm((2, 4, 4, 16, 768), BF16),
             vm((8, 2, 2, 3072), BF16),
             vm((8, 8, 128), I32),
             vm((32, 3072), F32),
-            vm((NCH, 2, 4, 4, 16, WH), BF16),
+            vm((2, 2, 4, 4, 16, 1536), BF16),
             vm((2, 2, 512, 256), BF16),
             vm((16, 3072), I32),
             vm((512, 3072), F32),
@@ -572,15 +551,14 @@
             vm((2, 4, 3072), F32),
             vm((2, 4, 3072), BF16),
             dma((6,)),
-            dma((8,)), dma((8,)),
-            dma((8,)), dma((8,)),
-            dma((2, 12)), dma((2, 12)),
-            dma((NCH, 12)), dma((NCH, 12)),
+            dma((2,)), dma((2,)),
+            dma((2,)), dma((2,)),
+            dma((2, 2)), dma((2, 2)),
             dma((5, 2)), dma((5, 2)),
-            dma((2, 16)), dma((2, 16)),
-            dma((2, 6)), dma((2, 6)),
-            dma((8,)), dma((8,)),
-            dma((2, 8)), dma((2, 8)),
+            dma((2,)), dma((2,)),
+            dma((2, 2)), dma((2, 2)),
+            dma((1,)), dma((1,)),
+            dma((2,)), dma((2,)),
         ],
         compiler_params=pltpu.CompilerParams(
             collective_id=0, has_side_effects=True, vmem_limit_bytes=56 * 1024 * 1024

time: 70.4 us -> 68.8 us (0.977)
  Pallas kernels: 68.1 us -> 66 us
    pallas_call x1, Pallas kernels: 68.1 us -> 66 us  [body(): pl.pallas_call(kernel, out_shape=[jax.ShapeDtypeStruct((16, 4, 3072), F32...]
where the time goes in v5:
time: 68.8 us; the launch traced here: 68.2 us
  Pallas kernels  66 us (96%)
  other arithmetic  2.18 us (3%)
    pallas_call x1, Pallas kernels, body(): pl.pallas_call(kernel, out_shape=[jax.ShapeDtypeStruct((16, 4, 3072), F32...  66 us
    add x1, other arithmetic, body(): return early + late.astype(F32)  2.18 us

profile of v5, /device:TPU:32, one launch (start us, length us, event | category | flops | bytes accessed | tf_op | source)
XLA Modules:
  0.0 68.2 jit_solution(14588936256246192169)
XLA Ops:
  0.0 66.0 %shard_map.73 = (f32[16,4,3072]{2,1,0:T(4,128)}, bf16[16,4,3072]{2,1,0:T(4,128)(2,1)}) custom-call(bf16[16,4,3072]{2,1,0:T(4,128)(2,1)} %img_hbm.1, f32[1,3072]{1,0:T(1,128)} %bitcast.7, bf16[3072,768]{1,0:T(8,128)(2,1)} %up_hbm.1, bf16[768,3072]{1,0:T(8,128)(2,1)} %dn_hbm.1, bf16[16,2,3072]{2,1,0:T(2,128)(2,1)} %cot_hbm.1, s32[2]{0:T(128)} %seeds_ref.1, ...), custom_call_target="tpu_custom_call" | custom-call | flops 8000000000 | bytes 12000000 | tf_op jit(solution)/shard_map/pallas_call | solution.py:500
  66.0 2.2 %convert_add_fusion = f32[8,8,3072]{2,1,0:T(8,128)} fusion(f32[8,8,3072]{2,1,0:T(8,128)} %bitcast.5, bf16[8,8,3072]{2,1,0:T(8,128)(2,1)} %bitcast.6), kind=kLoop, calls=%fused_computation | loop fusion | flops 393216 | bytes 1966080 | tf_op jit(solution)/shard_map/add | solution.py:568

commit v6 on v5

--- a/solution.py
+++ b/solution.py
@@ -131,8 +131,6 @@
     z_seed = Copies(live, z_send.at[0], z_recv.at[0], seedg.at[pl.ds(0, 7)], z_peer(1))
     z_cot = Copies(live, z_send.at[1], z_recv.at[1], rc.at[pl.ds(0, 7)], z_peer(1))
     for s in z_order:
-        z_seed.send(seedg.at[z], seedg.at[z], z_peer(s))
-    for s in z_order:
         z_cot.send(cot_hbm.at[pl.ds(2 * wrap(z + s, 8), 2)], rc.at[z], z_peer(s))
 
     class Gather:
@@ -157,6 +155,8 @@
     cot_g = [Gather(cg.at[j], c_send.at[j], c_recv.at[j]) for j in range(2)]
 
     img_g.start(1)
+    for s in z_order:
+        z_seed.send(seedg.at[z], seedg.at[z], z_peer(s))
 
     sub16 = lax.broadcasted_iota(I32, (16, 128), 0)
     lane = lax.broadcasted_iota(I32, (16, 128), 1)
@@ -475,9 +475,9 @@
     back_part(1)
     cp_bk[1].start()
     hidden(1)
-    finish(0)
     spread(1)
     sums_y(1)
+    finish(0)
     ea.wait_recv()
     ld_ea.wait()
     old = [cp for cp in live if cp is not parts[1] and cp is not sums[1, 1]]

time: 68.8 us -> 68.2 us (level)
  no operation moved by 1% of the time
where the time goes in v6:
time: 68.2 us; the launch traced here: 68 us
  Pallas kernels  65.8 us (96%)
  other arithmetic  2.18 us (3%)
    pallas_call x1, Pallas kernels, body(): pl.pallas_call(kernel, out_shape=[jax.ShapeDtypeStruct((16, 4, 3072), F32...  65.8 us
    add x1, other arithmetic, body(): return early + late.astype(F32)  2.18 us

profile of v6, /device:TPU:32, one launch (start us, length us, event | category | flops | bytes accessed | tf_op | source)
XLA Modules:
  0.0 68.0 jit_solution(2443340790971076258)
XLA Ops:
  0.0 65.8 %shard_map.73 = (f32[16,4,3072]{2,1,0:T(4,128)}, bf16[16,4,3072]{2,1,0:T(4,128)(2,1)}) custom-call(bf16[16,4,3072]{2,1,0:T(4,128)(2,1)} %img_hbm.1, f32[1,3072]{1,0:T(1,128)} %bitcast.7, bf16[3072,768]{1,0:T(8,128)(2,1)} %up_hbm.1, bf16[768,3072]{1,0:T(8,128)(2,1)} %dn_hbm.1, bf16[16,2,3072]{2,1,0:T(2,128)(2,1)} %cot_hbm.1, s32[2]{0:T(128)} %seeds_ref.1, ...), custom_call_target="tpu_custom_call" | custom-call | flops 8000000000 | bytes 12000000 | tf_op jit(solution)/shard_map/pallas_call | solution.py:500
  65.9 2.2 %convert_add_fusion = f32[8,8,3072]{2,1,0:T(8,128)} fusion(f32[8,8,3072]{2,1,0:T(8,128)} %bitcast.5, bf16[8,8,3072]{2,1,0:T(8,128)(2,1)} %bitcast.6), kind=kLoop, calls=%fused_computation | loop fusion | flops 393216 | bytes 1966080 | tf_op jit(solution)/shard_map/add | solution.py:568

commit v7 on v6

--- a/solution.py
+++ b/solution.py
@@ -263,8 +263,6 @@
             noisy[:, lo : lo + 768] = noisy[:, lo : lo + 768] + dot_nn(
                 onehot[ab, half], imgg[ab].reshape(256, 768)
             )
-    pump(1)
-
     def stat_blocks(k, carry):
         tot, m2 = carry
         for u in range(4):
@@ -311,6 +309,7 @@
                 pre[tok, h, :, n * 256 : (n + 1) * 256] = res[lo : lo + 128]
         ugp[:, n * 256 : (n + 1) * 256] = res[512:528]
 
+    pump(1)
     pre_cols(0)
     pre_cols(1)
     pre_cols(2)

time: 68.2 us -> 66.7 us (0.978)
  Pallas kernels: 65.8 us -> 64.3 us
    pallas_call x1, Pallas kernels: 65.8 us -> 64.3 us  [body(): pl.pallas_call(kernel, out_shape=[jax.ShapeDtypeStruct((16, 4, 3072), F32...]
where the time goes in v7:
time: 66.7 us; the launch traced here: 66.5 us
  Pallas kernels  64.3 us (96%)
  other arithmetic  2.18 us (3%)
    pallas_call x1, Pallas kernels, body(): pl.pallas_call(kernel, out_shape=[jax.ShapeDtypeStruct((16, 4, 3072), F32...  64.3 us
    add x1, other arithmetic, body(): return early + late.astype(F32)  2.18 us

profile of v7, /device:TPU:32, one launch (start us, length us, event | category | flops | bytes accessed | tf_op | source)
XLA Modules:
  0.0 66.5 jit_solution(15181905876818021144)
XLA Ops:
  0.0 64.3 %shard_map.73 = (f32[16,4,3072]{2,1,0:T(4,128)}, bf16[16,4,3072]{2,1,0:T(4,128)(2,1)}) custom-call(bf16[16,4,3072]{2,1,0:T(4,128)(2,1)} %img_hbm.1, f32[1,3072]{1,0:T(1,128)} %bitcast.7, bf16[3072,768]{1,0:T(8,128)(2,1)} %up_hbm.1, bf16[768,3072]{1,0:T(8,128)(2,1)} %dn_hbm.1, bf16[16,2,3072]{2,1,0:T(2,128)(2,1)} %cot_hbm.1, s32[2]{0:T(128)} %seeds_ref.1, ...), custom_call_target="tpu_custom_call" | custom-call | flops 8000000000 | bytes 12000000 | tf_op jit(solution)/shard_map/pallas_call | solution.py:499
  64.3 2.2 %convert_add_fusion = f32[8,8,3072]{2,1,0:T(8,128)} fusion(f32[8,8,3072]{2,1,0:T(8,128)} %bitcast.5, bf16[8,8,3072]{2,1,0:T(8,128)(2,1)} %bitcast.6), kind=kLoop, calls=%fused_computation | loop fusion | flops 393216 | bytes 1966080 | tf_op jit(solution)/shard_map/add | solution.py:567
